TPU v7x, 32 devices: a whole 2x2x4 slice. The times are simulated.
32 devices in a mesh: batch: 8 (over y, x, core), blk: 4 (over z).
Axes of the slice: x: 2, y: 2, z: 4, core: 2. Of those that a mesh axis runs over, the one named last changes fastest.
Arguments:
- tokens: bfloat16 [16, 1024, 1024], P('batch', 'blk'), may hold values from -6 to 6
- doc_starts: int32 [16, 8], P('batch'), may hold values from 0 to 1023, as said below
- attn_gain: bfloat16 [1024], replicated, may hold values from 0.5 to 1.5
- attn_shift: bfloat16 [1024], replicated, may hold values from -2 to 2
- qkv_weight: bfloat16 [1024, 3072], replicated, may hold values from -0.1875 to 0.1875
- qkv_bias: bfloat16 [3072], replicated, may hold values from -2 to 2
- query_down_factor: bfloat16 [1024, 4], replicated, may hold values from -0.1875 to 0.1875
- query_up_factor: bfloat16 [4, 1024], replicated, may hold values from -0.09375 to 0.09375
- value_down_factor: bfloat16 [1024, 4], replicated, may hold values from -0.1875 to 0.1875
- value_up_factor: bfloat16 [4, 1024], replicated, may hold values from -0.09375 to 0.09375
- out_weight: bfloat16 [1024, 1024], replicated, may hold values from -0.75 to 0.75
- out_bias: bfloat16 [1024], replicated, may hold values from -2 to 2
- mlp_gain: bfloat16 [1024], replicated, may hold values from 0.5 to 1.5
- mlp_shift: bfloat16 [1024], replicated, may hold values from -2 to 2
- fc_weight: bfloat16 [1024, 4096], replicated, may hold values from -0.1875 to 0.1875
- fc_bias: bfloat16 [4096], replicated, may hold values from -2 to 2
- proj_weight: bfloat16 [4096, 1024], replicated, may hold values from -0.09375 to 0.09375
- proj_bias: bfloat16 [1024], replicated, may hold values from -2 to 2
- out_grad: bfloat16 [16, 1024, 1024], P('batch', 'blk'), may hold values from -6 to 6
Outputs:
- block_out: bfloat16 [16, 1024, 1024], P('batch', 'blk')
- tokens_grad: bfloat16 [16, 1024, 1024], P('batch', 'blk')
- grad_down_query: float32 [1024, 4], replicated
- grad_up_query: float32 [4, 1024], replicated
- grad_down_value: float32 [1024, 4], replicated
- grad_up_value: float32 [4, 1024], replicated
Inputs may be any that keep to these rules, and one draw needn't show every extreme that they name: `doc_starts`: each slot holds 8 document starts, rising strictly, the first of them 0.
All inputs are finite; a program needn't handle non-finite values.
Results may differ from a plain program's by a relative error of at most 0.015.
Values may be sent and summed in bfloat16 or wider, within the bound.
A program may use at most 192 MiB of HBM per device.

v0:
```python
import math

import jax
import jax.numpy as jnp
from jax import lax
from jax.sharding import PartitionSpec as P

H = 16


epsilon = 1e-05
adapter_scale = 8.0
neg_big = -1e30
highest_precision = lax.Precision.HIGHEST


def layer_norm(value_rows, gain, shift):
    center = value_rows - jnp.mean(value_rows, -1, keepdims=True)
    inverse = lax.rsqrt(jnp.mean(center * center, -1, keepdims=True) + epsilon)
    normalized_input = center * inverse
    return (normalized_input * gain + shift, normalized_input, inverse)


def norm_back(upstream, normalized_input, inverse, gain):
    scaled = upstream * gain
    return inverse * (
        scaled
        - jnp.mean(scaled, -1, keepdims=True)
        - normalized_input * jnp.mean(scaled * normalized_input, -1, keepdims=True)
    )


def back_dot(left, weight):
    return lax.dot_general(
        left, weight, (((left.ndim - 1,), (1,)), ((), ())), preferred_element_type=jnp.float32
    )


def pairs(array):
    return array.reshape((array.shape[0] // 2, 2) + array.shape[1:])


def unpairs(array):
    return array.reshape((array.shape[0] * array.shape[1],) + array.shape[2:])


def heads_split(array):
    return array.reshape(array.shape[:-1] + (H, array.shape[-1] // H))


def doc_index(positions, starts):
    return jnp.sum((positions[:, :, None] >= starts[:, None, :]).astype(jnp.int32), -1)


def on_device(
    tokens,
    doc_starts,
    attn_gain,
    attn_shift,
    qkv_weight,
    qkv_bias,
    query_down_factor,
    query_up_factor,
    value_down_factor,
    value_up_factor,
    out_weight,
    out_bias,
    mlp_gain,
    mlp_shift,
    fc_weight,
    fc_bias,
    proj_weight,
    proj_bias,
    out_grad,
):
    slot_count, span_len, hidden_width = tokens.shape
    head_size = hidden_width // H
    score_scale = 1.0 / math.sqrt(head_size)
    full_len = span_len * lax.axis_size("blk")
    tokens_wide = tokens.astype(jnp.float32)
    attn_gain_wide = attn_gain.astype(jnp.float32)
    mlp_gain_wide = mlp_gain.astype(jnp.float32)
    normed_full, normed_one, inverse_one = layer_norm(
        tokens_wide, attn_gain_wide, attn_shift.astype(jnp.float32)
    )
    normed_low = normed_full.astype(jnp.bfloat16)
    projected_rows = jnp.dot(
        normed_low, qkv_weight, preferred_element_type=jnp.float32
    ) + qkv_bias.astype(jnp.float32)
    query_adapter_inner = jnp.dot(normed_low, query_down_factor, preferred_element_type=jnp.float32)
    value_adapter_inner = jnp.dot(normed_low, value_down_factor, preferred_element_type=jnp.float32)
    queries_low = (
        projected_rows[..., :hidden_width]
        + adapter_scale
        * jnp.dot(
            query_adapter_inner, query_up_factor.astype(jnp.float32), precision=highest_precision
        )
    ).astype(jnp.bfloat16)
    keys_low = projected_rows[..., hidden_width : 2 * hidden_width].astype(jnp.bfloat16)
    values_low = (
        projected_rows[..., 2 * hidden_width :]
        + adapter_scale
        * jnp.dot(
            value_adapter_inner, value_up_factor.astype(jnp.float32), precision=highest_precision
        )
    ).astype(jnp.bfloat16)
    own_pos = lax.axis_index("blk") * span_len + jnp.arange(span_len, dtype=jnp.int32)
    own_pos = jnp.broadcast_to(own_pos, (slot_count, span_len))
    all_pos = jnp.broadcast_to(jnp.arange(full_len, dtype=jnp.int32), (slot_count, full_len))

    def allowed_pair(query_pos, key_pos):
        query_doc = doc_index(query_pos, doc_starts)
        key_doc = doc_index(key_pos, doc_starts)
        return (key_doc[:, None, :] == query_doc[:, :, None]) & (
            key_pos[:, None, :] <= query_pos[:, :, None]
        )

    query_heads = heads_split(queries_low)

    def fold_keys(carry, pieces):
        key_piece, value_piece = pieces
        length = key_piece.shape[1]
        key_pos = jnp.broadcast_to(jnp.arange(length, dtype=jnp.int32), (slot_count, length))
        allowed = allowed_pair(own_pos, key_pos)

        def attend(operands):
            query_part, key_part, value_part, allow_part, top_old, total_old, accum_old = operands
            scores = (
                jnp.einsum(
                    "sqhd,skhd->shqk", query_part, key_part, preferred_element_type=jnp.float32
                )
                * score_scale
            )
            mask_four = allow_part[:, None, :, :]
            scores = jnp.where(mask_four, scores, neg_big)
            top_new = jnp.maximum(top_old, jnp.max(scores, -1))
            weights = jnp.where(mask_four, jnp.exp(scores - top_new[..., None]), 0.0)
            rescale = jnp.exp(top_old - top_new)
            total_new = total_old * rescale + jnp.sum(weights, -1)
            mixture = jnp.einsum(
                "shqk,skhd->sqhd",
                weights.astype(jnp.bfloat16),
                value_part,
                preferred_element_type=jnp.float32,
            )
            accum_new = accum_old * jnp.transpose(rescale, (0, 2, 1))[..., None] + mixture
            return (top_new, total_new, accum_new)

        operands = (
            pairs(query_heads),
            pairs(heads_split(key_piece)),
            pairs(heads_split(value_piece)),
            pairs(allowed),
        ) + tuple((pairs(item) for item in carry))
        results = lax.map(attend, operands)
        return tuple((unpairs(item) for item in results))

    start_state = (
        jnp.full((slot_count, H, span_len), neg_big, jnp.float32),
        jnp.zeros((slot_count, H, span_len), jnp.float32),
        jnp.zeros((slot_count, span_len, H, head_size), jnp.float32),
    )
    state = fold_keys(
        start_state,
        (
            lax.all_gather(keys_low, "blk", axis=1, tiled=True),
            lax.all_gather(values_low, "blk", axis=1, tiled=True),
        ),
    )
    top_fin, total_fin, accum_fin = state
    attended = (accum_fin / jnp.transpose(total_fin, (0, 2, 1))[..., None]).reshape(
        slot_count, span_len, hidden_width
    )
    log_total = top_fin + jnp.log(total_fin)
    attended_low = attended.astype(jnp.bfloat16)
    resid = tokens_wide + (
        jnp.dot(attended_low, out_weight, preferred_element_type=jnp.float32)
        + out_bias.astype(jnp.float32)
    )
    normed_mlp, normed_two, inverse_two = layer_norm(
        resid, mlp_gain_wide, mlp_shift.astype(jnp.float32)
    )
    normed_mlp_low = normed_mlp.astype(jnp.bfloat16)
    hidden = jnp.dot(
        normed_mlp_low, fc_weight, preferred_element_type=jnp.float32
    ) + fc_bias.astype(jnp.float32)

    def gelu_tanh(value_rows):
        return jax.nn.gelu(value_rows, approximate=True)

    activ, gelu_pull = jax.vjp(gelu_tanh, hidden)
    activ_low = activ.astype(jnp.bfloat16)
    block_out = (
        resid
        + (
            jnp.dot(activ_low, proj_weight, preferred_element_type=jnp.float32)
            + proj_bias.astype(jnp.float32)
        )
    ).astype(jnp.bfloat16)
    grad_activ = back_dot(out_grad, proj_weight)
    grad_hidden = gelu_pull(grad_activ)[0].astype(jnp.bfloat16)
    grad_normed_two = back_dot(grad_hidden, fc_weight)
    grad_resid = out_grad.astype(jnp.float32) + norm_back(
        grad_normed_two, normed_two, inverse_two, mlp_gain_wide
    )
    grad_attended = back_dot(grad_resid.astype(jnp.bfloat16), out_weight).astype(jnp.bfloat16)
    grad_att_heads = heads_split(grad_attended)
    row_delta = jnp.transpose(
        jnp.sum(grad_att_heads.astype(jnp.float32) * heads_split(attended), -1), (0, 2, 1)
    )
    keys_back, values_back = (
        lax.all_gather(keys_low, "blk", axis=1, tiled=True),
        lax.all_gather(values_low, "blk", axis=1, tiled=True),
    )

    def score_grads(
        query_part, key_part, value_part, allow_part, total_part, delta_part, grad_part
    ):
        scores = (
            jnp.einsum("sqhd,skhd->shqk", query_part, key_part, preferred_element_type=jnp.float32)
            * score_scale
        )
        mask_four = allow_part[:, None, :, :]
        weights = jnp.where(mask_four, jnp.exp(scores - total_part[..., None]), 0.0)
        grad_weights = jnp.einsum(
            "sqhd,skhd->shqk", grad_part, value_part, preferred_element_type=jnp.float32
        )
        grad_scores = (weights * (grad_weights - delta_part[..., None])).astype(jnp.bfloat16)
        return (weights, grad_scores)

    def both_side_grads(operands):
        weights, grad_scores = score_grads(*operands)
        grad_query = (
            jnp.einsum(
                "shqk,skhd->sqhd", grad_scores, operands[1], preferred_element_type=jnp.float32
            )
            * score_scale
        )
        grad_key = (
            jnp.einsum(
                "shqk,sqhd->skhd", grad_scores, operands[0], preferred_element_type=jnp.float32
            )
            * score_scale
        )
        grad_value = jnp.einsum(
            "shqk,sqhd->skhd",
            weights.astype(jnp.bfloat16),
            operands[6],
            preferred_element_type=jnp.float32,
        )
        return (grad_query, grad_key, grad_value)

    back_ops = (
        pairs(query_heads),
        pairs(heads_split(keys_back)),
        pairs(heads_split(values_back)),
        pairs(allowed_pair(own_pos, all_pos)),
        pairs(log_total),
        pairs(row_delta),
        pairs(grad_att_heads),
    )
    grad_query_h, grad_key_h, grad_value_h = (
        unpairs(item) for item in lax.map(both_side_grads, back_ops)
    )
    grad_key_all = grad_key_h.reshape(slot_count, full_len, hidden_width)
    grad_value_all = grad_value_h.reshape(slot_count, full_len, hidden_width)
    grad_key_own, grad_value_own = (
        lax.psum_scatter(
            grad_key_all.astype(jnp.bfloat16), "blk", scatter_dimension=1, tiled=True
        ).astype(jnp.float32),
        lax.psum_scatter(
            grad_value_all.astype(jnp.bfloat16), "blk", scatter_dimension=1, tiled=True
        ).astype(jnp.float32),
    )
    grad_keys = grad_key_own.astype(jnp.bfloat16)
    grad_values = grad_value_own.astype(jnp.bfloat16)
    grad_queries = grad_query_h.reshape(slot_count, span_len, hidden_width).astype(jnp.bfloat16)
    normed_wide = normed_low.astype(jnp.float32)
    query_adapter_lift = adapter_scale * jnp.einsum(
        "scd,rd->scr", grad_queries, query_up_factor, preferred_element_type=jnp.float32
    )
    value_adapter_lift = adapter_scale * jnp.einsum(
        "scd,rd->scr", grad_values, value_up_factor, preferred_element_type=jnp.float32
    )
    query_up_gradient = adapter_scale * jnp.einsum(
        "scr,scd->rd",
        query_adapter_inner,
        grad_queries.astype(jnp.float32),
        precision=highest_precision,
    )
    value_up_gradient = adapter_scale * jnp.einsum(
        "scr,scd->rd",
        value_adapter_inner,
        grad_values.astype(jnp.float32),
        precision=highest_precision,
    )
    grad_down_q = jnp.einsum(
        "scd,scr->dr", normed_wide, query_adapter_lift, precision=highest_precision
    )
    grad_down_v = jnp.einsum(
        "scd,scr->dr", normed_wide, value_adapter_lift, precision=highest_precision
    )
    grad_project = jnp.concatenate([grad_queries, grad_keys, grad_values], -1)
    grad_normed_one = (
        back_dot(grad_project, qkv_weight)
        + jnp.einsum(
            "scr,dr->scd",
            query_adapter_lift,
            query_down_factor.astype(jnp.float32),
            precision=highest_precision,
        )
        + jnp.einsum(
            "scr,dr->scd",
            value_adapter_lift,
            value_down_factor.astype(jnp.float32),
            precision=highest_precision,
        )
    )
    tokens_grad = (
        grad_resid + norm_back(grad_normed_one, normed_one, inverse_one, attn_gain_wide)
    ).astype(jnp.bfloat16)
    summed = lax.psum(
        (grad_down_q, query_up_gradient, grad_down_v, value_up_gradient), ("batch", "blk")
    )
    return (block_out, tokens_grad, summed[0], summed[1], summed[2], summed[3])


def solution(mesh):
    return jax.shard_map(
        on_device,
        mesh=mesh,
        in_specs=(
            P("batch", "blk", None),
            P("batch", None),
            P(),
            P(),
            P(),
            P(),
            P(),
            P(),
            P(),
            P(),
            P(),
            P(),
            P(),
            P(),
            P(),
            P(),
            P(),
            P(),
            P("batch", "blk", None),
        ),
        out_specs=(P("batch", "blk", None), P("batch", "blk", None), P(), P(), P(), P()),
        check_vma=False,
    )
```

profile of v0, /device:TPU:0, one launch (start us, length us, event | category | flops | bytes accessed | tf_op | source)
XLA Modules:
  0.0 572.4 jit_solution(9727638482528710885)
XLA Ops:
  12.6 6.1 %fusion.30 = f32[2,256,3072]{2,1,0:T(8,128)S(1)} fusion(bf16[1024,3072]{1,0:T(8,128)(2,1)} %param.23, f32[3072]{0:T(1024)S(1)} %convert_element_type.134, bf16[2,256,1024]{2,1,0:T(8,128)(2,1)} %param.19, f32[1024]{0:T(1024)S(1)} %convert_element_type.132, f32[1024]{0:T(1024)S(1)} %convert_element_type.131, f32[2,256]{1,0:T(2,128)S(1)} %add_rsqrt_fusion.1, ...), kind=kOutput, calls=%fused_computation.34 | convolution fusion | flops 3225944064 | bytes 13656064 | tf_op jit(solution)/shard_map/dot_general | solution.py:87
  24.0 3.7 fusion.59
  28.5 3.7 fusion.60
  36.5 69.6 %all-gather.3.cloned.1.call-done = bf16[2,1024,1024]{2,1,0:T(8,128)(2,1)} async-done(((bf16[2,256,1024]{2,1,0:T(8,128)(2,1)}), bf16[2,1024,1024]{2,1,0:T(8,128)(2,1)}) %all-gather.3.cloned.1.call-update) | async-done | bytes 4194320 | tf_op jit(solution)/shard_map/all_gather | solution.py:166
  106.1 6.2 %copy.49 = bf16[2,1024,1024]{1,2,0:T(8,128)(2,1)} copy(bf16[2,1024,1024]{2,1,0:T(8,128)(2,1)} %all-gather.3.cloned.1.call-done) | data formatting | bytes 8388608 | tf_op jit(solution)/shard_map/all_gather | solution.py:166
  112.3 16.5 %select_reduce_fusion = (f32[2,16,256]{2,1,0:T(8,128)S(1)}, f32[2,16,256,1024]{3,2,1,0:T(8,128)}) fusion(pred[2,256,1024]{2,1,0:T(8,128)(4,1)} %fusion.66, bf16[2,256,16,64]{1,3,2,0:T(8,128)(2,1)} %bitcast.127, bf16[2,1024,16,64]{1,3,2,0:T(8,128)(2,1)} %bitcast.121), kind=kOutput, calls=%fused_computation.3 | convolution fusion | flops 1098899456 | bytes 39354368 | tf_op jit(solution)/shard_map/while/body/eval_jaxpr/sqhd,skhd->shqk/dot_general | solution.py:129
  128.8 15.7 %fusion.1 = f32[2,16,256]{2,1,0:T(8,128)S(1)} fusion(f32[2,16,256,1024]{3,2,1,0:T(8,128)} %get-tuple-element.63, f32[2,16,256]{2,1,0:T(8,128)S(1)} %broadcast_maximum_fusion, pred[2,256,1024]{2,1,0:T(8,128)(4,1)S(1)} %copy-done.8), kind=kLoop, calls=%fused_computation.5 | loop fusion | flops 41934848 | bytes 34144256 | tf_op jit(solution)/shard_map/while/body/eval_jaxpr/reduce_sum | solution.py:139
  144.6 42.4 %all-gather.5.cloned.1.call-done = bf16[2,1024,1024]{2,1,0:T(8,128)(2,1)} async-done(((bf16[2,256,1024]{2,1,0:T(8,128)(2,1)}), bf16[2,1024,1024]{2,1,0:T(8,128)(2,1)}) %all-gather.5.cloned.1.call-update) | async-done | bytes 4194320 | tf_op jit(solution)/shard_map/all_gather | solution.py:167
  187.0 6.2 %copy.50 = bf16[2,1024,1024]{1,2,0:T(8,128)(2,1)} copy(bf16[2,1024,1024]{2,1,0:T(8,128)(2,1)} %all-gather.5.cloned.1.call-done) | data formatting | bytes 8388608 | tf_op jit(solution)/shard_map/all_gather | solution.py:167
  193.2 17.6 %fusion.116 = (bf16[2,256,16,64]{1,3,2,0:T(8,128)(2,1)}, f32[2,256,16,64]{1,3,2,0:T(8,128)}) fusion(f32[2,256,16]{1,2,0:T(8,128)S(1)} %bitcast_add_fusion.1, bf16[2,1024,16,64]{1,3,2,0:T(8,128)(2,1)} %bitcast.131, f32[2,16,256,1024]{3,2,1,0:T(8,128)} %get-tuple-element.63, f32[2,16,256]{2,1,0:T(8,128)S(1)} %broadcast_maximum_fusion, ...), kind=kOutput, calls=%fused_computation.139 | convolution fusion | flops 1117257728 | bytes 41517056 | tf_op jit(solution)/shard_map/while/body/eval_jaxpr/shqk,skhd->sqhd/dot_general | solution.py:140
  213.8 10.9 %fusion.22 = f32[2,256,4096]{2,1,0:T(8,128)} fusion(bf16[1024,4096]{1,0:T(8,128)(2,1)} %param.33, f32[2,256,1024]{2,1,0:T(8,128)S(1)} %get-tuple-element.78, f32[1024]{0:T(1024)S(1)} %convert_element_type.142, f32[1024]{0:T(1024)S(1)} %convert_element_type.141, f32[2,256]{1,0:T(2,128)S(1)} %add_rsqrt_fusion, f32[2,256]{1,0:T(2,128)S(1)} %broadcast_multiply_fusion.4), kind=kOutput, calls=%fused_computation.26 | convolution fusion | flops 4297588736 | bytes 18886656 | tf_op jit(solution)/shard_map/dot_general | solution.py:184
  224.7 15.3 %fusion.15 = bf16[2,256,4096]{2,1,0:T(8,128)(2,1)} fusion(f32[2,256,4096]{2,1,0:T(8,128)} %fusion.22, bf16[2,256,1024]{2,1,0:T(8,128)(2,1)S(1)} %copy-done.14, bf16[4096,1024]{1,0:T(8,128)(2,1)} %param.35, f32[4096]{0:T(1024)S(1)} %convert_element_type.144), kind=kOutput, calls=%fused_computation.19 | convolution fusion | flops 4339007488 | bytes 22036480 | tf_op jit(solution)/shard_map/dot_general | solution.py:34
  240.0 6.7 %multiply_reduce_fusion.3 = (f32[2,256]{1,0:T(2,128)S(1)}, f32[2,256]{1,0:T(2,128)S(1)}, f32[2,256,1024]{2,1,0:T(8,128)S(1)}) fusion(f32[1024]{0:T(1024)S(1)} %convert_element_type.141, f32[2,256]{1,0:T(2,128)S(1)} %add_rsqrt_fusion, f32[2,256,1024]{2,1,0:T(8,128)S(1)} %get-tuple-element.78, f32[2,256]{1,0:T(2,128)S(1)} %broadcast_multiply_fusion.4, ...), kind=kOutput, calls=%fused_computation.84 | convolution fusion | flops 4298112000 | bytes 16789504 | tf_op jit(solution)/shard_map/dot_general | solution.py:34
  252.3 16.6 %fusion.43 = bf16[2,16,64,1024]{3,2,1,0:T(8,128)(2,1)} fusion(bf16[2,256,16,64]{1,3,2,0:T(8,128)(2,1)S(1)} %bitcast.129, f32[2,16,256,1024]{3,2,1,0:T(8,128)} %get-tuple-element.63, f32[2,16,256]{2,1,0:T(8,128)S(1)} %get-tuple-element.60, pred[2,256,1024]{2,1,0:T(8,128)(4,1)} %fusion.66), kind=kOutput, calls=%fused_computation.48 | convolution fusion | flops 1109393408 | bytes 39354368 | tf_op jit(solution)/shard_map/while/body/eval_jaxpr/shqk,sqhd->skhd/dot_general | solution.py:245
  268.9 6.2 %copy.54 = bf16[2,1024,1024]{2,1,0:T(8,128)(2,1)} copy(bf16[2,1024,1024]{1,2,0:T(8,128)(2,1)} %bitcast.133) | data formatting | bytes 8388608 | tf_op jit(solution)/shard_map/convert_element_type | solution.py:272
  277.2 23.7 %multiply_convert_fusion = bf16[2,16,256,1024]{3,2,1,0:T(8,128)(2,1)} fusion(f32[2,16,256,1024]{3,2,1,0:T(8,128)} %get-tuple-element.63, bf16[2,256,16,64]{1,3,2,0:T(8,128)(2,1)} %bitcast.130, bf16[2,1024,16,64]{1,3,2,0:T(8,128)(2,1)} %bitcast.132, f32[2,16,256]{2,1,0:T(8,128)S(1)} %bitcast.135, f32[2,16,256]{2,1,0:T(8,128)S(1)} %get-tuple-element.60, ...), kind=kOutput, calls=%fused_computation | convolution fusion | flops 1124073472 | bytes 56164352 | tf_op jit(solution)/shard_map/while/body/eval_jaxpr/sqhd,skhd->shqk/dot_general | solution.py:225
  300.9 10.8 %multiply_convert_fusion.1 = bf16[2,16,64,1024]{3,2,1,0:T(8,128)(2,1)} fusion(bf16[2,256,16,64]{1,3,2,0:T(8,128)(2,1)S(1)} %bitcast.128, bf16[2,16,256,1024]{3,2,1,0:T(8,128)(2,1)} %multiply_convert_fusion), kind=kOutput, calls=%fused_computation.28 | convolution fusion | flops 1077936128 | bytes 22020096 | tf_op jit(solution)/shard_map/while/body/eval_jaxpr/shqk,sqhd->skhd/dot_general | solution.py:240
  311.7 6.2 %copy.53 = bf16[2,1024,1024]{2,1,0:T(8,128)(2,1)} copy(bf16[2,1024,1024]{1,2,0:T(8,128)(2,1)} %bitcast.123) | data formatting | bytes 8388608 | tf_op jit(solution)/shard_map/convert_element_type | solution.py:269
  318.6 12.3 %multiply_convert_fusion.4 = bf16[2,16,64,256]{3,2,1,0:T(8,128)(2,1)S(1)} fusion(bf16[2,1024,16,64]{1,3,2,0:T(8,128)(2,1)} %bitcast.122, bf16[2,16,256,1024]{3,2,1,0:T(8,128)(2,1)} %multiply_convert_fusion), kind=kOutput, calls=%fused_computation.74 | convolution fusion | flops 1074790400 | bytes 22020096 | tf_op jit(solution)/shard_map/while/body/eval_jaxpr/shqk,skhd->sqhd/dot_general | solution.py:234
  340.5 12.3 %add_convert_fusion = bf16[2,256,1024]{2,1,0:T(8,128)(2,1)} fusion(f32[2,256,1024]{2,1,0:T(8,128)S(1)} %copy-done.3, bf16[4096,1024]{1,0:T(8,128)(2,1)} %param.35, f32[2,256,4096]{2,1,0:T(8,128)} %fusion.22, f32[4096]{0:T(1024)S(1)} %convert_element_type.144, f32[1024]{0:T(1024)S(1)} %convert_element_type.146), kind=kOutput, calls=%fused_computation.78 | convolution fusion | flops 4317511680 | bytes 19943424 | tf_op jit(solution)/shard_map/dot_general | solution.py:196
  358.4 71.7 %reduce-scatter.3.cloned.1.call-done = bf16[2,256,1024]{2,1,0:T(8,128)(2,1)} async-done(((bf16[2,1024,1024]{2,1,0:T(8,128)(2,1)}), bf16[2,256,1024]{2,1,0:T(8,128)(2,1)}) %reduce-scatter.3.cloned.1.call-update) | async-done | bytes 1048592 | tf_op jit(solution)/shard_map/reduce_scatter | solution.py:268
  430.1 9.3 %fusion.115 = (f32[2,256]{1,0:T(2,128)S(1)}, f32[2,256]{1,0:T(2,128)S(1)}, f32[2,256,1024]{2,1,0:T(8,128)}) fusion(f32[2,256]{1,0:T(2,128)S(1)} %copy-done.31, f32[2,256]{1,0:T(2,128)S(1)} %copy-done.25, bf16[2,256,1024]{2,1,0:T(8,128)(2,1)S(1)} %copy-done.4, f32[1024]{0:T(1024)S(1)} %copy-done.34, f32[2,256,1024]{2,1,0:T(8,128)} %fusion.90, ...), kind=kOutput, calls=%fused_computation.138 | convolution fusion | flops 3235380224 | bytes 16789504 | tf_op jit(solution)/shard_map/dot_general | solution.py:34
  440.6 4.7 fusion.57
  445.3 115.0 %all-reduce.3.cloned.1.call-done = (f32[1024,4]{0,1:T(4,128)}, f32[4,1024]{1,0:T(4,128)}, f32[1024,4]{0,1:T(4,128)}, f32[4,1024]{1,0:T(4,128)}) async-done(((f32[1024,4]{0,1:T(4,128)}, f32[4,1024]{1,0:T(4,128)}, f32[1024,4]{0,1:T(4,128)}, f32[4,1024]{1,0:T(4,128)}), (f32[1024,4]{0,1:T(4,128)}, f32[4,1024]{1,0:T(4,128)}, f32[1024,4]{0,1:T(4,128)}, f32[4,1024]{1,0:T(4,128)})) %all-reduce.3.cloned.1.call-update) | async-done | bytes 65552 | tf_op jit(solution)/shard_map/psum | solution.py:322
  (146 shorter events, 48.4 us)
Async XLA Ops:
  7.2 203.7 %copy-start = (bf16[1024,1024]{1,0:T(8,128)(2,1)S(1)}, bf16[1024,1024]{1,0:T(8,128)(2,1)}, u32[]{:S(2)}) copy-start(bf16[1024,1024]{1,0:T(8,128)(2,1)} %param.29) | copy-start | bytes 6291460
  7.2 98.9 %all-gather.3.cloned.1.call-start = ((), (), s32[]{:S(2)}) async-start(), calls=%async_computation.2 | async-start | bytes 5242880 | tf_op jit(solution)/shard_map/all_gather | solution.py:166
  8.7 19.1 %copy-start.35 = (f32[1024]{0:T(1024)}, f32[1024]{0:T(1024)S(1)}, u32[]{:S(2)}) copy-start(f32[1024]{0:T(1024)S(1)} %convert_element_type.132) | copy-start | bytes 12292
  9.4 18.4 %copy-start.33 = (f32[1024]{0:T(1024)}, f32[1024]{0:T(1024)S(1)}, u32[]{:S(2)}) copy-start(f32[1024]{0:T(1024)S(1)} %convert_element_type.131) | copy-start | bytes 12292
  10.9 17.0 %copy-start.24 = (f32[2,256]{1,0:T(2,128)}, f32[2,256]{1,0:T(2,128)S(1)}, u32[]{:S(2)}) copy-start(f32[2,256]{1,0:T(2,128)S(1)} %broadcast_multiply_fusion.5) | copy-start | bytes 6148
  12.5 15.3 %copy-start.30 = (f32[2,256]{1,0:T(2,128)}, f32[2,256]{1,0:T(2,128)S(1)}, u32[]{:S(2)}) copy-start(f32[2,256]{1,0:T(2,128)S(1)} %add_rsqrt_fusion.1) | copy-start | bytes 6148
  22.5 164.5 %all-gather.5.cloned.1.call-start = ((), (), s32[]{:S(2)}) async-start(), calls=%async_computation.3 | async-start | bytes 5242880 | tf_op jit(solution)/shard_map/all_gather | solution.py:167
  27.7 325.1 %reduce-scatter.5.cloned.1.call-start = ((), (), s32[]{:S(2)}) async-start(), calls=%async_computation.5 | async-start | bytes 5242880 | tf_op jit(solution)/shard_map/reduce_scatter | solution.py:271
  28.4 83.9 %copy-start.22 = (f32[2,256,4]{1,2,0:T(4,128)}, f32[2,256,4]{1,2,0:T(4,128)S(1)}, u32[]{:S(2)}) copy-start(f32[2,256,4]{1,2,0:T(4,128)S(1)} %fusion.98) | copy-start | bytes 24580
  112.3 16.5 %copy-start.8 = (pred[2,256,1024]{2,1,0:T(8,128)(4,1)S(1)}, pred[2,256,1024]{2,1,0:T(8,128)(4,1)}, u32[]{:S(2)}) copy-start(pred[2,256,1024]{2,1,0:T(8,128)(4,1)} %fusion.66) | copy-start | bytes 1572868
  213.4 33.4 %copy-start.2 = (f32[2,256,1024]{2,1,0:T(8,128)}, f32[2,256,1024]{2,1,0:T(8,128)S(1)}, u32[]{:S(2)}) copy-start(f32[2,256,1024]{2,1,0:T(8,128)S(1)} %get-tuple-element.78) | copy-start | bytes 6291460
  213.8 10.9 %copy-start.14 = (bf16[2,256,1024]{2,1,0:T(8,128)(2,1)S(1)}, bf16[2,256,1024]{2,1,0:T(8,128)(2,1)}, u32[]{:S(2)}) copy-start(bf16[2,256,1024]{2,1,0:T(8,128)(2,1)} %param.37) | copy-start | bytes 3145732
  213.8 26.2 %slice-start = ((s8[8388608]{0:T(1024)(128)(4,1)}), s8[4194304]{0:T(1024)(128)(4,1)S(1)}, s32[]{:S(2)}) async-start(s8[8388608]{0:T(1024)(128)(4,1)} %bitcast.136), calls=%async_computation.7 | async-start | bytes 8388608
  224.7 15.3 %slice-start.1 = ((s8[8388608]{0:T(1024)(128)(4,1)}), s8[4194304]{0:T(1024)(128)(4,1)S(1)}, s32[]{:S(2)}) async-start(s8[8388608]{0:T(1024)(128)(4,1)} %bitcast.136), calls=%async_computation.8 | async-start | bytes 8388608
  252.3 22.9 %copy-start.11 = (bf16[2,256,1024]{1,2,0:T(8,128)(2,1)}, bf16[2,256,1024]{1,2,0:T(8,128)(2,1)S(1)}, u32[]{:S(2)}) copy-start(bf16[2,256,1024]{1,2,0:T(8,128)(2,1)S(1)} %copy.52) | copy-start | bytes 3145732
  275.1 155.0 %reduce-scatter.3.cloned.1.call-start = ((), (), s32[]{:S(2)}) async-start(), calls=%async_computation.4 | async-start | bytes 5242880 | tf_op jit(solution)/shard_map/reduce_scatter | solution.py:268
  277.2 23.7 %copy-start.7 = (bf16[2,256,1024]{1,2,0:T(8,128)(2,1)S(1)}, bf16[2,256,1024]{1,2,0:T(8,128)(2,1)}, u32[]{:S(2)}) copy-start(bf16[2,256,1024]{1,2,0:T(8,128)(2,1)} %copy.48) | copy-start | bytes 3145732
  318.0 242.4 %all-reduce.3.cloned.1.call-start = ((), (), s32[]{:S(2)}) async-start(), calls=%async_computation.6 | async-start | bytes 131072 | tf_op jit(solution)/shard_map/psum | solution.py:322
  318.6 14.8 %copy-start.17 = (bf16[4,1024]{1,0:T(4,128)(2,1)S(1)}, bf16[4,1024]{1,0:T(4,128)(2,1)}, u32[]{:S(2)}) copy-start(bf16[4,1024]{1,0:T(4,128)(2,1)} %param.26) | copy-start | bytes 24580
  340.5 12.3 %copy-start.19 = (bf16[4,1024]{1,0:T(4,128)(2,1)S(1)}, bf16[4,1024]{1,0:T(4,128)(2,1)}, u32[]{:S(2)}) copy-start(bf16[4,1024]{1,0:T(4,128)(2,1)} %param.28) | copy-start | bytes 24580
  352.8 77.3 %copy-start.15 = (bf16[2,256,1024]{2,1,0:T(8,128)(2,1)S(1)}, bf16[2,256,1024]{2,1,0:T(8,128)(2,1)}, u32[]{:S(2)}) copy-start(bf16[2,256,1024]{2,1,0:T(8,128)(2,1)} %copy.55) | copy-start | bytes 3145732
  352.8 77.3 %copy-start.12 = (bf16[2,256,1024]{2,1,0:T(8,128)(2,1)S(1)}, bf16[2,256,1024]{2,1,0:T(8,128)(2,1)}, u32[]{:S(2)}) copy-start(bf16[2,256,1024]{2,1,0:T(8,128)(2,1)} %reduce-scatter.5.cloned.1.call-done) | copy-start | bytes 3145732
  358.4 81.0 %copy-start.21 = (f32[2,256,4]{1,2,0:T(4,128)S(1)}, f32[2,256,4]{1,2,0:T(4,128)}, u32[]{:S(2)}) copy-start(f32[2,256,4]{1,2,0:T(4,128)} %copy-done.20) | copy-start | bytes 24580
  440.6 125.1 %copy-start.1 = (bf16[1024,1024]{1,0:T(8,128)(2,1)S(1)}, bf16[1024,1024]{1,0:T(8,128)(2,1)}, u32[]{:S(2)}) copy-start(bf16[1024,1024]{1,0:T(8,128)(2,1)} %param.29) | copy-start | bytes 6291460
  (25 other events, 96.9 us)
Sparse Core Ops, SparseCore 0:
  22.6 83.4 all-gather.2
  107.7 79.2 all-gather.4
  275.2 75.2 reduce-scatter.4
  352.8 77.2 reduce-scatter.2
  440.7 119.6 all-reduce.2
where the time goes:
time: 579 us; the launch traced here: 572 us
  waiting for transfers between devices  299 us (52%)
  matrix products  186 us (32%)
  local copies, waits for them, and re-layouts  43.6 us (8%)
  other arithmetic  29.7 us (5%)
  between operations  14.5 us (3%)
    psum x1, waiting for transfers between devices, on_device(): lax.psum((grad_down_q, query_up_gradient, grad_down_v, value_up_gradient)...  115 us
    reduce_scatter x1, waiting for transfers between devices, on_device(): lax.psum_scatter(grad_key_all.astype(jnp.bfloat16), 'blk', scatter_dimens...  71.7 us
    all_gather x1, waiting for transfers between devices, on_device(): lax.all_gather(keys_low, 'blk', axis=1, tiled=True)  69.6 us
    all_gather x1, waiting for transfers between devices, on_device(): lax.all_gather(values_low, 'blk', axis=1, tiled=True)  42.4 us
    dot_general x4, matrix products, back_dot(): lax.dot_general(left, weight, (((left.ndim - 1,), (1,)), ((), ())), prefe...  34 us
    dot_general x1, matrix products, score_grads(): jnp.einsum('sqhd,skhd->shqk', grad_part, value_part, preferred_element_ty...  23.7 us
    dot_general x1, matrix products, attend(): jnp.einsum('shqk,skhd->sqhd', weights.astype(jnp.bfloat16), value_part, p...  17.6 us
    dot_general x1, matrix products, both_side_grads(): jnp.einsum('shqk,sqhd->skhd', weights.astype(jnp.bfloat16), operands[6],...  16.6 us
  transfers between devices with their start and end apart: 5, of which 4 were waited for; matrix products, arithmetic and copies ran while one was open for 24% of the time, Pallas kernels for 0%

commit v1 on v0

v1 whole, which is shorter than its diff:
```python
import jax
import jax.numpy as jnp
from jax import lax
from jax.experimental import pallas as pl
from jax.experimental.pallas import tpu as pltpu
from jax.sharding import PartitionSpec as P

F32 = jnp.float32
BF = jnp.bfloat16
MESH = pl.DeviceIdType.MESH
EPS = 1e-05
ADAPTER = 8.0
NEG = -1e30
LOG2E = 1.4426950408889634
LN2 = 0.6931471805599453
HEAD = 64
PAIR = 128
NN = (((1,), (0,)), ((), ()))
NT = (((1,), (1,)), ((), ()))
TN = (((0,), (0,)), ((), ()))


def dot(a, b, dims=NN):
    return lax.dot_general(a, b, dims, preferred_element_type=F32)


def row(ref):
    return ref[...].astype(F32).reshape(1, ref.shape[0])


def places():
    batch = lax.axis_index("batch")
    z = lax.axis_index("blk")
    core = lax.rem(batch, 2)
    base = batch - core
    outer = lax.rem(core + z, 2)
    edge = 1 - lax.rem((z + 1) // 2, 2)
    low, high = 1 - outer, 2 + outer
    hosts = [(base + lax.rem(i + edge, 2), 2 * core + i) for i in (0, 1)]
    homes = [(base + z // 2, low), (base + z // 2, high)]
    mate = (base + 1 - core, z)
    return dict(
        batch=batch, z=z, core=core, outer=outer, low=low, high=high,
        hosts=hosts, homes=homes, mate=mate,
    )


def greet(devices):
    barrier = pltpu.get_barrier_semaphore()
    for device in devices:
        pl.semaphore_signal(barrier, inc=1, device_id=device, device_id_type=MESH)
    pl.semaphore_wait(barrier, len(devices))


def remote(src, dst, send, recv, device):
    return pltpu.make_async_remote_copy(
        src_ref=src, dst_ref=dst, send_sem=send, recv_sem=recv,
        device_id=device, device_id_type=MESH,
    )


def norm_stats(x):
    center = x - jnp.mean(x, -1, keepdims=True)
    inverse = lax.rsqrt(jnp.mean(center * center, -1, keepdims=True) + EPS)
    return center * inverse, inverse


def norm_back(upstream, normed, inverse, gain):
    scaled = upstream * gain
    return inverse * (
        scaled
        - jnp.mean(scaled, -1, keepdims=True)
        - normed * jnp.mean(scaled * normed, -1, keepdims=True)
    )


def mask_bias(starts, key_span, query_span, span):
    key_pos = lax.broadcasted_iota(jnp.int32, (span, 1), 0) + key_span * span
    query_pos = lax.broadcasted_iota(jnp.int32, (1, span), 1) + query_span * span
    key_doc = jnp.zeros((span, 1), jnp.int32)
    query_doc = jnp.zeros((1, span), jnp.int32)
    for j in range(starts.shape[1]):
        start = starts[0:1, j : j + 1]
        key_doc = key_doc + (key_pos >= start).astype(jnp.int32)
        query_doc = query_doc + (query_pos >= start).astype(jnp.int32)
    allowed = (key_doc == query_doc) & (key_pos <= query_pos)
    return jnp.where(allowed, 0.0, NEG)


def half_rows(x, head):
    part = x[HEAD * head : HEAD * head + HEAD]
    zero = jnp.zeros_like(part)
    return jnp.concatenate([part, zero] if head == 0 else [zero, part], 0)


def half_lanes(x, head):
    lane = lax.broadcasted_iota(jnp.int32, x.shape, 1)
    keep = (lane < HEAD) if head == 0 else (lane >= HEAD)
    return jnp.where(keep, x, jnp.zeros_like(x))


def front_kernel(
    tok, og, wqkv, starts, gain, shift, qkv_bias, down_q, up_q, down_v, up_v,
    tok_o, og_o, q_o, k_o, v_o, e_o, ot_o, on_o, wf_o, rl_o,
    tokin, wf, n1, qn, kn, vn, qp, vt, sc, ee, bias, ot, on, starts_in,
    tok_s, tok_r, og_s, og_r, ex_s, ex_r, st_sem, loc, e_sem,
):
    at = places()
    z, core, outer = at["z"], at["core"], at["outer"]
    span, width = tokin.shape[1], tokin.shape[2]
    pairs_n = qn.shape[0]
    blocks = width // 256

    load_w = pltpu.make_async_copy(wqkv, wf, loc.at[0])
    load_w.start()
    greet(at["hosts"] + at["homes"] + [at["mate"]])
    tok_send = [
        remote(tok.at[i], tokin.at[z // 2], tok_s.at[i], tok_r.at[z // 2], at["hosts"][i])
        for i in (0, 1)
    ]
    for copy in tok_send:
        copy.start()
    starts_copy = remote(starts, starts_in, st_sem.at[0], st_sem.at[1], at["mate"])
    starts_copy.start()

    load_w.wait()
    for part, down, up in ((0, down_q, up_q), (2, down_v, up_v)):

        @pl.loop(0, blocks)
        def _(c):
            col = pl.ds(pl.multiple_of(part * width + c * 256, 256), 256)
            here = pl.ds(pl.multiple_of(c * 256, 256), 256)
            extra = dot(down[...], up[:, here])
            wf[:, col] = (wf[:, col].astype(F32) + ADAPTER * extra).astype(BF)

    save_w = pltpu.make_async_copy(wf, wf_o, loc.at[0])
    save_w.start()

    starts_copy.wait()
    mine = (z // 2 == core).astype(jnp.int32)
    both = starts[...] * mine + starts_in[...] * (1 - mine)
    second = lax.rem(z, 2)
    chosen = both[0:1] * (1 - second) + both[1:2] * second
    low, high = at["low"], at["high"]
    first_remote = 1 - low
    key_spans = (low, high, low, first_remote, first_remote + outer)
    query_spans = (low, high, high, low + outer * (high - low), high)
    for j in range(5):
        bias[j] = mask_bias(chosen, key_spans[j], query_spans[j], span)

    for i in (0, 1):
        remote(tokin.at[i], tokin.at[i], tok_s.at[i], tok_r.at[i], at["mate"]).wait_recv()
        x = tokin[i].astype(F32)
        normed, _ = norm_stats(x)
        n1[pl.ds(i * span, span), :] = (normed * row(gain) + row(shift)).astype(BF)
    for copy in tok_send:
        copy.wait_send()
    og_send = [
        remote(og.at[i], og_o.at[z // 2], og_s.at[i], og_r.at[z // 2], at["hosts"][i])
        for i in (0, 1)
    ]
    for copy in og_send:
        copy.start()
    save_tok = pltpu.make_async_copy(tokin, tok_o, loc.at[1])
    save_tok.start()

    def exchange(c):
        here = pl.ds(2 * c, 2)
        return [
            remote(ref.at[here, 0:2], ref.at[here, 2:4], ex_s.at[c, t], ex_r.at[c, t], at["mate"])
            for t, ref in enumerate((kn, vn))
        ]

    biases = row(qkv_bias)

    @pl.loop(0, blocks)
    def _(c):
        for part, store, scale in ((1, kn, None), (2, vn, None), (0, qn, LOG2E / HEAD**0.5)):
            col = pl.ds(pl.multiple_of(part * width + c * 256, 256), 256)
            made = dot(n1[...], wf[:, col]) + qkv_bias[col].astype(F32).reshape(1, 256)
            if scale is not None:
                made = made * scale
            made = made.astype(BF)
            for s in (0, 1):
                for t in (0, 1):
                    store[2 * c + t, s] = made[s * span : (s + 1) * span, t * PAIR : (t + 1) * PAIR]
            if part == 2:
                for copy in exchange(c):
                    copy.start()

    outer_f = outer.astype(F32)
    inner_f = 1.0 - outer_f
    ones = jnp.ones((16, span), BF)

    def save_e(hp):
        return pltpu.make_async_copy(ee.at[lax.rem(hp, 2)], e_o.at[hp], e_sem.at[lax.rem(hp, 2)])

    @pl.loop(0, pairs_n)
    def _(hp):
        slot = lax.rem(hp, 2)

        @pl.when(slot == 0)
        def _():
            for copy in exchange(hp // 2):
                copy.wait()

        @pl.when(hp >= 2)
        def _():
            save_e(hp - 2).wait()

        for s in (0, 1):
            q_t = qn[hp, s].T
            for head in (0, 1):
                qp[head, s] = half_rows(q_t, head)
        for kb in range(4):
            vt[kb] = vn[hp, kb].T
        key_at = (0, 1, 0, 2, 2 + outer)
        query_at = (0, 1, 1, outer, 1)
        tops = []
        for head in (0, 1):
            tops.append([])
            for j in range(5):
                s_j = dot(kn[hp, key_at[j]], qp[head, query_at[j]]) + bias[j]
                sc[head, j] = s_j
                tops[head].append(jnp.max(s_j, 0, keepdims=True))
        for head in (0, 1):
            m0, m1, m2, m3, m4 = tops[head]
            top_low = jnp.maximum(m0, m3 * inner_f + NEG * outer_f)
            top_high = jnp.maximum(
                jnp.maximum(m1, m2), jnp.maximum(m4, m3 * outer_f + NEG * inner_f)
            )
            top_x = top_high * outer_f + top_low * inner_f
            mixed = []
            for j, top in enumerate((top_low, top_high, top_high, top_x, top_high)):
                e_j = jnp.exp2(sc[head, j] - top).astype(BF)
                ee[slot, head * 5 + j] = e_j
                v_j = jnp.concatenate(
                    [vt[key_at[j], HEAD * head : HEAD * head + HEAD], ones], 0
                )
                mixed.append(dot(v_j, e_j))
            sums = (
                mixed[0] + mixed[3] * inner_f,
                mixed[1] + mixed[2] + mixed[4] + mixed[3] * outer_f,
            )
            for s in (0, 1):
                inv = 1.0 / sums[s][HEAD : HEAD + 1]
                rl_o[hp, 2 * head + s : 2 * head + s + 1, :] = inv
                ot[hp, s, HEAD * head : HEAD * head + HEAD, :] = (sums[s][:HEAD] * inv).astype(BF)
        for s in (0, 1):
            on[s, :, pl.ds(pl.multiple_of(hp * PAIR, PAIR), PAIR)] = ot[hp, s].T
        save_e(hp).start()

    outs = [
        pltpu.make_async_copy(src, dst, loc.at[k + 2])
        for k, (src, dst) in enumerate(((on, on_o), (ot, ot_o), (qn, q_o), (kn, k_o), (vn, v_o)))
    ]
    for copy in outs:
        copy.start()
    for hp in (pairs_n - 2, pairs_n - 1):
        save_e(hp).wait()
    for copy in outs:
        copy.wait()
    save_w.wait()
    save_tok.wait()
    for i in (0, 1):
        og_send[i].wait_send()
        remote(og_o.at[i], og_o.at[i], og_s.at[i], og_r.at[i], at["mate"]).wait_recv()


def mlp_kernel(
    on, tok, og, wo, out_bias, gain, shift, proj_bias, fc_bias, fc, proj,
    out, gr, da,
    resid, n2, acc_o, acc_g, og_flat,
):
    step = pl.program_id(0)
    span = tok.shape[1]

    @pl.when(step == 0)
    def _():
        for s in (0, 1):
            here = pl.ds(s * span, span)
            r = tok[s].astype(F32) + (dot(on[s], wo[...]) + row(out_bias))
            resid[here] = r
            normed, _ = norm_stats(r)
            n2[here] = (normed * row(gain) + row(shift)).astype(BF)
            acc_o[here] = r + row(proj_bias)
            acc_g[here] = jnp.zeros_like(r)
            og_flat[here] = og[s]

    x = dot(n2[...], fc[...]) + row(fc_bias)
    sq = x * x
    k0 = 0.7978845608028654
    t = jnp.tanh(x * (k0 + (k0 * 0.044715) * sq))
    half = 0.5 + 0.5 * t
    act = (x * half).astype(BF)
    slope = half + 0.5 * x * (1.0 - t * t) * (k0 + (3.0 * k0 * 0.044715) * sq)
    acc_o[...] += dot(act, proj[...])
    gh = (dot(og_flat[...], proj[...], NT) * slope).astype(BF)
    acc_g[...] += dot(gh, fc[...], NT)

    @pl.when(step == pl.num_programs(0) - 1)
    def _():
        for s in (0, 1):
            here = pl.ds(s * span, span)
            out[s] = acc_o[here].astype(BF)
            normed, inverse = norm_stats(resid[here])
            g = og[s].astype(F32) + norm_back(acc_g[here], normed, inverse, row(gain))
            gr[s] = g
            da[s] = dot(g.astype(BF), wo[...], NT).astype(BF)


def back_kernel(
    rounds,
    out_h, gr, da, tok, q_h, k_h, v_h, ot_h, e_h, wf_h, rl, gain, shift, down_q, up_q, down_v, up_v,
    out_o, tg_o, gdq_o, guq_o, gdv_o, guv_o,
    qn, kn, vn, ot, ee, wf, da_s, tok_s, gr_s, dq, dk, dv, kt, dop, don, qm, part, part_in, gn, tg, n1,
    ar, ar_in,
    out_s, out_r, tg_s, tg_r, ex_s, ex_r, ar_s, ar_r, loc, e_sem,
):
    at = places()
    z, outer = at["z"], at["outer"]
    span, width = tg.shape[1], tg.shape[2]
    pairs_n = qn.shape[0]
    batch = at["batch"]
    peers = []
    for axis, distance in rounds:
        if axis == 0:
            low_bit = lax.rem(batch // distance, 2)
            peers.append((batch + distance - 2 * distance * low_bit, z))
        else:
            low_bit = lax.rem(z // distance, 2)
            peers.append((batch, z + distance - 2 * distance * low_bit))

    def load_e(hp):
        return pltpu.make_async_copy(e_h.at[hp], ee.at[lax.rem(hp, 2)], e_sem.at[lax.rem(hp, 2)])

    loads = [
        pltpu.make_async_copy(src, dst, loc.at[k])
        for k, (src, dst) in enumerate(
            ((da, da_s), (ot_h, ot), (q_h, qn), (k_h, kn), (v_h, vn), (wf_h, wf), (tok, tok_s), (gr, gr_s))
        )
    ]
    for copy in loads[:5]:
        copy.start()
    load_e(0).start()
    for copy in loads[5:]:
        copy.start()
    greet(at["hosts"] + at["homes"] + [at["mate"]] + peers)
    out_send = [
        remote(out_h.at[i], out_o.at[lax.rem(z, 2)], out_s.at[i], out_r.at[lax.rem(z, 2)], at["homes"][i])
        for i in (0, 1)
    ]
    for copy in out_send:
        copy.start()
    for copy in loads[:5]:
        copy.wait()

    outer_f = outer.astype(F32)
    inner_f = 1.0 - outer_f
    key_at = (0, 1, 0, 2, 2 + outer)
    query_at = (0, 1, 1, outer, 1)

    def exchange(hp):
        return remote(part.at[hp], part_in.at[hp], ex_s.at[hp], ex_r.at[hp], at["mate"])

    @pl.loop(0, pairs_n)
    def _(hp):
        slot = lax.rem(hp, 2)
        lanes = pl.ds(pl.multiple_of(hp * PAIR, PAIR), PAIR)

        @pl.when(hp + 1 < pairs_n)
        def _():
            load_e(hp + 1).start()

        load_e(hp).wait()
        delta = [[None, None], [None, None]]
        for s in (0, 1):
            da_t = da_s[s, :, lanes].astype(F32).T
            o_t = ot[hp, s].astype(F32)
            prod = da_t * o_t
            scaled = []
            for head in (0, 1):
                rows_h = slice(HEAD * head, HEAD * head + HEAD)
                inv = rl[hp, 2 * head + s : 2 * head + s + 1, :]
                delta[head][s] = jnp.sum(prod[rows_h], 0, keepdims=True) * inv
                scaled.append(da_t[rows_h] * inv)
            both = jnp.concatenate(scaled, 0).astype(BF)
            natural = both.T
            q_n = qn[hp, s]
            for head in (0, 1):
                dop[head, s] = half_rows(both, head)
                don[s, head * span : (head + 1) * span] = half_lanes(natural, head)
                qm[s, head * span : (head + 1) * span] = half_lanes(q_n, head)
        for kb in range(4):
            kt[kb] = kn[hp, kb].T
        dq_t = [[None, None], [None, None]]
        grads = [[], []]
        dk_parts, dv_parts = [], []
        for j in range(5):
            ds_pair, e_pair = [], []
            for head in (0, 1):
                d_low, d_high = delta[head]
                d_j = (d_low, d_high, d_high, d_high * outer_f + d_low * inner_f, d_high)[j]
                e_j = ee[slot, head * 5 + j]
                dp = dot(vn[hp, key_at[j]], dop[head, query_at[j]])
                ds_j = (e_j.astype(F32) * (dp - d_j)).astype(BF)
                grads[head].append(
                    dot(kt[key_at[j], HEAD * head : HEAD * head + HEAD], ds_j)
                )
                ds_pair.append(ds_j)
                e_pair.append(e_j)
            dk_parts.append(dot(jnp.concatenate(ds_pair, 1), qm[query_at[j]]))
            dv_parts.append(dot(jnp.concatenate(e_pair, 1), don[query_at[j]]))
        for t, parts, scale in ((0, dk_parts, LN2), (1, dv_parts, 1.0)):
            store = (dk, dv)[t]
            store[0, :, lanes] = ((parts[0] + parts[2]) * scale).astype(BF)
            store[1, :, lanes] = (parts[1] * scale).astype(BF)
            part[hp, t, 0] = ((parts[3] + parts[4] * inner_f) * scale).astype(BF)
            part[hp, t, 1] = (parts[4] * (outer_f * scale)).astype(BF)
        exchange(hp).start()
        for s in (0, 1):
            rows_t = []
            for head in (0, 1):
                g = grads[head]
                if s == 0:
                    total = g[0] + g[3] * inner_f
                else:
                    total = g[1] + g[2] + g[4] + g[3] * outer_f
                rows_t.append(total * (1.0 / HEAD**0.5))
            dq[s, :, lanes] = jnp.concatenate(rows_t, 0).astype(BF).T

    @pl.loop(0, pairs_n)
    def _(hp):
        lanes = pl.ds(pl.multiple_of(hp * PAIR, PAIR), PAIR)
        exchange(hp).wait()
        for t, store in ((0, dk), (1, dv)):
            for s in (0, 1):
                mine = store[s, :, lanes].astype(F32)
                store[s, :, lanes] = (mine + part_in[hp, t, s].astype(F32)).astype(BF)

    for copy in loads[5:]:
        copy.wait()
    tg_send = []
    for s in (0, 1):

        @pl.loop(0, width // 256)
        def _(c):
            here = pl.ds(pl.multiple_of(c * 256, 256), 256)
            total = dot(dq[s], wf[here, 0:width], NT)
            total += dot(dk[s], wf[here, width : 2 * width], NT)
            total += dot(dv[s], wf[here, 2 * width : 3 * width], NT)
            gn[:, here] = total

        normed, inverse = norm_stats(tok_s[s].astype(F32))
        n1[s] = (normed * row(gain) + row(shift)).astype(BF)
        tg[s] = (gr_s[s] + norm_back(gn[...], normed, inverse, row(gain))).astype(BF)
        if s == 0:
            for i in (0, 1):
                out_send[i].wait_send()
        copy = remote(
            tg.at[s], tg_o.at[lax.rem(z, 2)], tg_s.at[s], tg_r.at[lax.rem(z, 2)], at["homes"][s]
        )
        copy.start()
        tg_send.append(copy)

    ar[...] = jnp.zeros_like(ar)
    for k, (grad, down, up) in enumerate(((dq, down_q, up_q), (dv, down_v, up_v))):
        up_total = down_total = 0.0
        for s in (0, 1):
            inner = dot(n1[s], down[...]).astype(BF)
            lift = dot(grad[s], up[...], NT).astype(BF)
            up_total = up_total + dot(inner, grad[s], TN)
            down_total = down_total + dot(lift, n1[s], TN)
        ar[2 * k, 0:4] = ADAPTER * up_total
        ar[2 * k + 1, 0:4] = ADAPTER * down_total
    for r, peer in enumerate(peers):
        copy = remote(ar, ar_in.at[r], ar_s.at[r], ar_r.at[r], peer)
        copy.start()
        copy.wait()
        ar[...] += ar_in[r]
    guq_o[...] = ar[0, 0:4]
    guv_o[...] = ar[2, 0:4]
    gdq_o[...] = ar[1].T[:, 0:4]
    gdv_o[...] = ar[3].T[:, 0:4]

    for i in (0, 1):
        remote(out_o.at[i], out_o.at[i], out_s.at[i], out_r.at[i], at["mate"]).wait_recv()
        tg_send[i].wait_send()
        remote(tg_o.at[i], tg_o.at[i], tg_s.at[i], tg_r.at[i], at["mate"]).wait_recv()


VMEM = pl.BlockSpec(memory_space=pltpu.VMEM)
ANY = pl.BlockSpec(memory_space=pl.ANY)
DMA = pltpu.SemaphoreType.DMA
LIMIT = 60 * 1024 * 1024


def on_device(
    tokens, doc_starts, attn_gain, attn_shift, qkv_weight, qkv_bias,
    query_down_factor, query_up_factor, value_down_factor, value_up_factor,
    out_weight, out_bias, mlp_gain, mlp_shift, fc_weight, fc_bias, proj_weight, proj_bias, out_grad,
):
    slots, span, width = tokens.shape
    hidden = fc_weight.shape[1]
    rank = query_down_factor.shape[1]
    pairs_n = width // PAIR
    shape = jax.ShapeDtypeStruct
    rows_two = shape((slots, span, width), BF)
    q_shape = (pairs_n, 2, span, PAIR)
    k_shape = (pairs_n, 4, span, PAIR)
    e_shape = (pairs_n, 10, span, span)
    t_shape = (pairs_n, 2, PAIR, span)

    tok, og, q_h, k_h, v_h, e_h, ot, on, wf, rl = pl.pallas_call(
        front_kernel,
        out_shape=(
            rows_two, rows_two, shape(q_shape, BF), shape(k_shape, BF), shape(k_shape, BF),
            shape(e_shape, BF), shape(t_shape, BF), rows_two, shape((width, 3 * width), BF),
            shape((pairs_n, 8, span), F32),
        ),
        in_specs=[ANY] * 3 + [VMEM] * 8,
        out_specs=(ANY,) * 9 + (VMEM,),
        scratch_shapes=[
            pltpu.VMEM((2, span, width), BF),
            pltpu.VMEM((width, 3 * width), BF),
            pltpu.VMEM((2 * span, width), BF),
            pltpu.VMEM(q_shape, BF),
            pltpu.VMEM(k_shape, BF),
            pltpu.VMEM(k_shape, BF),
            pltpu.VMEM((2, 2, PAIR, span), BF),
            pltpu.VMEM((4, PAIR, span), BF),
            pltpu.VMEM((2, 5, span, span), F32),
            pltpu.VMEM((2, 10, span, span), BF),
            pltpu.VMEM((5, span, span), F32),
            pltpu.VMEM(t_shape, BF),
            pltpu.VMEM((2, span, width), BF),
            pltpu.VMEM(doc_starts.shape, jnp.int32),
            DMA((2,)), DMA((2,)), DMA((2,)), DMA((2,)),
            DMA((width // 256, 2)), DMA((width // 256, 2)), DMA((2,)), DMA((7,)), DMA((2,)),
        ],
        compiler_params=pltpu.CompilerParams(
            collective_id=0, has_side_effects=True, vmem_limit_bytes=LIMIT
        ),
    )(
        tokens, out_grad, qkv_weight, doc_starts, attn_gain, attn_shift, qkv_bias,
        query_down_factor, query_up_factor, value_down_factor, value_up_factor,
    )

    chunk = 512
    whole = lambda *dims: pl.BlockSpec(dims, lambda f: (0,) * len(dims))
    out_slot, grad_resid, grad_att = pl.pallas_call(
        mlp_kernel,
        grid=(hidden // chunk,),
        out_shape=(rows_two, shape((slots, span, width), F32), rows_two),
        in_specs=[
            whole(slots, span, width), whole(slots, span, width), whole(slots, span, width),
            whole(width, width), whole(width), whole(width), whole(width), whole(width),
            pl.BlockSpec((chunk,), lambda f: (f,)),
            pl.BlockSpec((width, chunk), lambda f: (0, f)),
            pl.BlockSpec((chunk, width), lambda f: (f, 0)),
        ],
        out_specs=(whole(slots, span, width),) * 3,
        scratch_shapes=[
            pltpu.VMEM((2 * span, width), F32),
            pltpu.VMEM((2 * span, width), BF),
            pltpu.VMEM((2 * span, width), F32),
            pltpu.VMEM((2 * span, width), F32),
            pltpu.VMEM((2 * span, width), BF),
        ],
        compiler_params=pltpu.CompilerParams(
            dimension_semantics=("arbitrary",), vmem_limit_bytes=LIMIT
        ),
    )(on, tok, og, out_weight, out_bias, mlp_gain, mlp_shift, proj_bias, fc_bias, fc_weight, proj_weight)

    rounds = []
    for axis, size in ((0, lax.axis_size("batch")), (1, lax.axis_size("blk"))):
        distance = 1
        while distance < size:
            rounds.append((axis, distance))
            distance *= 2
    n_rounds = len(rounds)

    def back(*refs):
        back_kernel(rounds, *refs)

    small = lambda *dims: shape(dims, F32)
    return pl.pallas_call(
        back,
        out_shape=(
            rows_two, rows_two, small(width, rank), small(rank, width), small(width, rank), small(rank, width),
        ),
        in_specs=[ANY] * 10 + [VMEM] * 7,
        out_specs=(ANY,) * 2 + (VMEM,) * 4,
        scratch_shapes=[
            pltpu.VMEM(q_shape, BF),
            pltpu.VMEM(k_shape, BF),
            pltpu.VMEM(k_shape, BF),
            pltpu.VMEM(t_shape, BF),
            pltpu.VMEM((2, 10, span, span), BF),
            pltpu.VMEM((width, 3 * width), BF),
            pltpu.VMEM((2, span, width), BF),
            pltpu.VMEM((2, span, width), BF),
            pltpu.VMEM((2, span, width), F32),
            pltpu.VMEM((2, span, width), BF),
            pltpu.VMEM((2, span, width), BF),
            pltpu.VMEM((2, span, width), BF),
            pltpu.VMEM((4, PAIR, span), BF),
            pltpu.VMEM((2, 2, PAIR, span), BF),
            pltpu.VMEM((2, 2 * span, PAIR), BF),
            pltpu.VMEM((2, 2 * span, PAIR), BF),
            pltpu.VMEM((pairs_n, 2, 2, span, PAIR), BF),
            pltpu.VMEM((pairs_n, 2, 2, span, PAIR), BF),
            pltpu.VMEM((span, width), F32),
            pltpu.VMEM((2, span, width), BF),
            pltpu.VMEM((2, span, width), BF),
            pltpu.VMEM((4, 8, width), F32),
            pltpu.VMEM((n_rounds, 4, 8, width), F32),
            DMA((2,)), DMA((2,)), DMA((2,)), DMA((2,)), DMA((pairs_n,)), DMA((pairs_n,)),
            DMA((n_rounds,)), DMA((n_rounds,)), DMA((8,)), DMA((2,)),
        ],
        compiler_params=pltpu.CompilerParams(
            collective_id=1, has_side_effects=True, vmem_limit_bytes=LIMIT
        ),
    )(
        out_slot, grad_resid, grad_att, tok, q_h, k_h, v_h, ot, e_h, wf, rl, attn_gain, attn_shift,
        query_down_factor, query_up_factor, value_down_factor, value_up_factor,
    )


def solution(mesh):
    rows = P("batch", "blk", None)
    return jax.shard_map(
        on_device,
        mesh=mesh,
        in_specs=(rows, P("batch", None)) + (P(),) * 16 + (rows,),
        out_specs=(rows, rows, P(), P(), P(), P()),
        check_vma=False,
    )
```

time: 579 us -> 163 us (0.28); the launches traced: 572 us -> 162 us
  waiting for transfers between devices: 299 us -> 0 us
  matrix products: 186 us -> 0 us
  Pallas kernels: 0 us -> 148 us
  other arithmetic: 29.7 us -> 0 us
  local copies, waits for them, and re-layouts: 43.6 us -> 14 us
  between operations: 14.5 us -> 0.65 us
    dot_general x26 -> x0, matrix products: 186 us -> none  [the longest x4 34 us: back_dot(): lax.dot_general(left, weight, (((left.ndim - 1,), (1,)), ((), ())), prefe...]
    pallas_call x0 -> x3, Pallas kernels: none -> 148 us  [the longest x1 69.2 us: on_device(): pl.pallas_call(back, out_shape=(rows_two, rows_two, small(width, rank), s...]
    psum x1 -> x0, waiting for transfers between devices: 115 us -> none  [on_device(): lax.psum((grad_down_q, query_up_gradient, grad_down_v, value_up_gradient)...]
    all_gather x2 -> x0, waiting for transfers between devices: 112 us -> none  [the longest x1 69.6 us: on_device(): lax.all_gather(keys_low, 'blk', axis=1, tiled=True)]
    reduce_scatter x2 -> x0, waiting for transfers between devices: 71.7 us -> none  [the longest x1 71.7 us: on_device(): lax.psum_scatter(grad_key_all.astype(jnp.bfloat16), 'blk', scatter_dimens...]
    reduce_sum x7 -> x0, other arithmetic: 21.3 us -> none  [the longest x1 15.7 us: attend(): total_new = total_old * rescale + jnp.sum(weights, -1)]
    convert_element_type x5 -> x0, local copies, waits for them, and re-layouts: 18.1 us -> none  [the longest x1 6.23 us: on_device(): grad_key_all.astype(jnp.bfloat16)]
    all_gather x2 -> x0, local copies, waits for them, and re-layouts: 12.4 us -> none  [the longest x1 6.21 us: on_device(): lax.all_gather(keys_low, 'blk', axis=1, tiled=True)]
  transfers between devices with their start and end apart: 5 -> 0, of which waited for: 4 -> 0; matrix products, arithmetic and copies ran while one was open for 24% -> 0% of each run, Pallas kernels for 0% -> 0%
where the time goes in v1:
time: 163 us; the launch traced here: 162 us
  Pallas kernels  148 us (91%)
  local copies, waits for them, and re-layouts  14 us (9%)
    pallas_call x1, Pallas kernels, on_device(): pl.pallas_call(back, out_shape=(rows_two, rows_two, small(width, rank), s...  69.2 us
    pallas_call x1, Pallas kernels, on_device(): pl.pallas_call(front_kernel, out_shape=(rows_two, rows_two, shape(q_shape...  48.1 us
    pallas_call x1, Pallas kernels, on_device(): pl.pallas_call(mlp_kernel, grid=(hidden // chunk,), out_shape=(rows_two,...  30.3 us
    unnamed x6, local copies, waits for them, and re-layouts  10.3 us
    pallas_call x2, local copies, waits for them, and re-layouts, on_device(): pl.pallas_call(back, out_shape=(rows_two, rows_two, small(width, rank), s...  3.67 us

profile of v1, /device:TPU:0, one launch (start us, length us, event | category | flops | bytes accessed | tf_op | source)
XLA Modules:
  0.0 162.3 jit_solution(12180837966248362356)
XLA Ops:
  0.6 1.6 copy.25.down_q.refs_13_
  2.2 1.6 copy.26.down_v.refs_15_
  3.8 48.1 %shard_map.226 = (bf16[2,256,1024]{2,1,0:T(8,128)(2,1)}, bf16[2,256,1024]{2,1,0:T(8,128)(2,1)}, bf16[8,2,256,128]{3,2,1,0:T(8,128)(2,1)}, bf16[8,4,256,128]{3,2,...) custom-call(bf16[2,256,1024]{2,1,0:T(8,128)(2,1)} %tok.1, ...), custom_call_target="tpu_custom_call" | custom-call | tf_op jit(solution)/shard_map/pallas_call | solution.py:514
  51.9 30.3 %shard_map.227 = (bf16[2,256,1024]{2,1,0:T(8,128)(2,1)}, f32[2,256,1024]{2,1,0:T(8,128)}, bf16[2,256,1024]{2,1,0:T(8,128)(2,1)}) custom-call(bf16[2,256,1024]{2,1,0:T(8,128)(2,1)} %get-tuple-element.19.on, bf16[2,256,1024]{2,1,0:T(8,128)(2,1)} %get-tuple-element.20.tok.refs_3_, bf16[2,256,1024]{2,1,0:T(8,128)(2,1)} %get-tuple-element.21.og, ...), custom_call_target="tpu_custom_call" | custom-call | tf_op jit(solution)/shard_map/pallas_call | solution.py:551
  82.2 69.2 %shard_map.228 = (bf16[2,256,1024]{2,1,0:T(8,128)(2,1)}, bf16[2,256,1024]{2,1,0:T(8,128)(2,1)}, f32[1024,4]{1,0:T(8,128)}, f32[4,1024]{1,0:T(4,128)}, f32[1024,4]{1,0:T(8,128)}, /*index=5*/f32[4,1024]{1,0:T(4,128)}) custom-call(bf16[2,256,1024]{2,1,0:T(8,128)(2,1)} %get-tuple-element.22.refs_0_, f32[2,256,1024]{2,1,0:T(8,128)} %get-tuple-element.23.refs_1_, ...), custom_call_target="tpu_custom_call" | custom-call | tf_op jit(solution)/shard_map/pallas_call | solution.py:587
  151.5 1.8 %copy.29 = f32[1024,4]{0,1:T(4,128)} copy(f32[1024,4]{1,0:T(8,128)} %get-tuple-element.34) | data formatting | bytes 32768 | tf_op jit(solution)/shard_map/pallas_call | solution.py:587
  153.3 1.8 %copy.30 = f32[1024,4]{0,1:T(4,128)} copy(f32[1024,4]{1,0:T(8,128)} %get-tuple-element.36) | data formatting | bytes 32768 | tf_op jit(solution)/shard_map/pallas_call | solution.py:587
  155.2 2.3 %copy.35 = bf16[2,256,1024]{2,1,0:T(8,128)(2,1)} copy(bf16[2,256,1024]{2,1,0:T(8,128)(2,1)} %get-tuple-element.44) | data formatting | bytes 2097152
  157.4 2.3 %copy.36 = bf16[2,256,1024]{2,1,0:T(8,128)(2,1)} copy(bf16[2,256,1024]{2,1,0:T(8,128)(2,1)} %get-tuple-element.45) | data formatting | bytes 2097152
  159.7 1.3 copy.37
  161.0 1.3 copy.38

commit v2 on v1

v2 whole, which is shorter than its diff:
```python
import jax
import jax.numpy as jnp
from jax import lax
from jax.experimental import pallas as pl
from jax.experimental.pallas import tpu as pltpu
from jax.sharding import PartitionSpec as P

F32 = jnp.float32
BF = jnp.bfloat16
MESH = pl.DeviceIdType.MESH
EPS = 1e-05
ADAPTER = 8.0
NEG = -1e30
LOG2E = 1.4426950408889634
LN2 = 0.6931471805599453
HEAD = 64
PAIR = 128
NN = (((1,), (0,)), ((), ()))
NT = (((1,), (1,)), ((), ()))
TN = (((0,), (0,)), ((), ()))


def dot(a, b, dims=NN):
    return lax.dot_general(a, b, dims, preferred_element_type=F32)


def row(ref):
    return ref[...].astype(F32).reshape(1, ref.shape[0])


def places():
    batch = lax.axis_index("batch")
    z = lax.axis_index("blk")
    core = lax.rem(batch, 2)
    base = batch - core
    outer = lax.rem(core + z, 2)
    edge = 1 - lax.rem((z + 1) // 2, 2)
    low, high = 1 - outer, 2 + outer
    hosts = [(base + lax.rem(i + edge, 2), 2 * core + i) for i in (0, 1)]
    homes = [(base + z // 2, low), (base + z // 2, high)]
    mate = (base + 1 - core, z)
    return dict(
        batch=batch, z=z, core=core, outer=outer, low=low, high=high,
        hosts=hosts, homes=homes, mate=mate,
    )


def greet(devices):
    barrier = pltpu.get_barrier_semaphore()
    for device in devices:
        pl.semaphore_signal(barrier, inc=1, device_id=device, device_id_type=MESH)
    pl.semaphore_wait(barrier, len(devices))


def remote(src, dst, send, recv, device):
    return pltpu.make_async_remote_copy(
        src_ref=src, dst_ref=dst, send_sem=send, recv_sem=recv,
        device_id=device, device_id_type=MESH,
    )


def norm_stats(x):
    center = x - jnp.mean(x, -1, keepdims=True)
    inverse = lax.rsqrt(jnp.mean(center * center, -1, keepdims=True) + EPS)
    return center * inverse, inverse


def norm_back(upstream, normed, inverse, gain):
    scaled = upstream * gain
    return inverse * (
        scaled
        - jnp.mean(scaled, -1, keepdims=True)
        - normed * jnp.mean(scaled * normed, -1, keepdims=True)
    )


def mask_bias(starts, key_span, query_span, span):
    key_pos = lax.broadcasted_iota(jnp.int32, (span, 1), 0) + key_span * span
    query_pos = lax.broadcasted_iota(jnp.int32, (1, span), 1) + query_span * span
    key_doc = jnp.zeros((span, 1), jnp.int32)
    query_doc = jnp.zeros((1, span), jnp.int32)
    for j in range(starts.shape[1]):
        start = starts[0:1, j : j + 1]
        key_doc = key_doc + (key_pos >= start).astype(jnp.int32)
        query_doc = query_doc + (query_pos >= start).astype(jnp.int32)
    allowed = (key_doc == query_doc) & (key_pos <= query_pos)
    return jnp.where(allowed, 0.0, NEG)


def half_rows(x, head):
    part = x[HEAD * head : HEAD * head + HEAD]
    zero = jnp.zeros_like(part)
    return jnp.concatenate([part, zero] if head == 0 else [zero, part], 0)


def half_lanes(x, head):
    lane = lax.broadcasted_iota(jnp.int32, x.shape, 1)
    keep = (lane < HEAD) if head == 0 else (lane >= HEAD)
    return jnp.where(keep, x, jnp.zeros_like(x))


def fused_kernel(
    rounds,
    tok, og, wqkv, wo_h, fc_h, proj_h, starts, gain, shift, qkv_bias, out_bias, gain2, shift2,
    fc_bias, proj_bias, down_q, up_q, down_v, up_v,
    out_o, tg_o, sums_o, e_h,
    tokin, ogin, wf, wo, fcb, pjb, n1, n2, qn, kn, vn, qp, vt, sc, ee, bias, ot, on, rl,
    resid, acc, slope, outst, dk, dv, dopc, don, qm, dss, part, part_in, tg, ar, ar_in, starts_in,
    tok_s, tok_r, og_s, og_r, ex_s, ex_r, st_sem, w_sem, fc_sem, pj_sem, e_sem,
    out_s, out_r, tg_s, tg_r, px_s, px_r, ar_s, ar_r,
):
    at = places()
    z, core, outer = at["z"], at["core"], at["outer"]
    low, high, mate, batch = at["low"], at["high"], at["mate"], at["batch"]
    span, width = tokin.shape[1], tokin.shape[2]
    pairs_n = qn.shape[0]
    blocks = width // 256
    chunks, chunk = slope.shape[0], slope.shape[2]
    peers = []
    for axis, distance in rounds:
        if axis == 0:
            bit = lax.rem(batch // distance, 2)
            peers.append((batch + distance - 2 * distance * bit, z))
        else:
            bit = lax.rem(z // distance, 2)
            peers.append((batch, z + distance - 2 * distance * bit))

    load_w = pltpu.make_async_copy(wqkv, wf, w_sem.at[0])
    load_w.start()
    greet(at["hosts"] + at["homes"] + [mate] + peers)
    tok_send = [
        remote(tok.at[i], tokin.at[z // 2], tok_s.at[i], tok_r.at[z // 2], at["hosts"][i])
        for i in (0, 1)
    ]
    for copy in tok_send:
        copy.start()
    starts_copy = remote(starts, starts_in, st_sem.at[0], st_sem.at[1], mate)
    starts_copy.start()

    def load_mlp(c):
        slot = lax.rem(c, 2)
        here = pl.ds(pl.multiple_of(c * chunk, chunk), chunk)
        return (
            pltpu.make_async_copy(fc_h.at[:, here], fcb.at[slot], fc_sem.at[slot]),
            pltpu.make_async_copy(proj_h.at[here, :], pjb.at[slot], pj_sem.at[slot]),
        )

    load_w.wait()
    load_o = pltpu.make_async_copy(wo_h, wo, w_sem.at[0])
    load_o.start()
    for c in (0, 1):
        for copy in load_mlp(c):
            copy.start()
    for part_w, down, up in ((0, down_q, up_q), (2, down_v, up_v)):

        @pl.loop(0, blocks)
        def _(c):
            col = pl.ds(pl.multiple_of(part_w * width + c * 256, 256), 256)
            here = pl.ds(pl.multiple_of(c * 256, 256), 256)
            extra = dot(down[...], up[:, here], TN)
            wf[:, col] = (wf[:, col].astype(F32) + ADAPTER * extra).astype(BF)

    starts_copy.wait()
    mine = (z // 2 == core).astype(jnp.int32)
    both = starts[...] * mine + starts_in[...] * (1 - mine)
    second = lax.rem(z, 2)
    chosen = both[0:1] * (1 - second) + both[1:2] * second
    first_remote = 1 - low
    key_spans = (low, high, low, first_remote, first_remote + outer)
    query_spans = (low, high, high, low + outer * (high - low), high)
    for j in range(5):
        bias[j] = mask_bias(chosen, key_spans[j], query_spans[j], span)

    def exchange(s, c):
        here = pl.ds(2 * c, 2)
        return [
            remote(ref.at[here, s], ref.at[here, 2 + s], ex_s.at[s, c, t], ex_r.at[s, c, t], mate)
            for t, ref in enumerate((kn, vn))
        ]

    for turn in (0, 1):
        s = z // 2 if turn == 0 else 1 - z // 2
        remote(tokin.at[s], tokin.at[s], tok_s.at[0], tok_r.at[s], mate).wait_recv()
        if turn == 1:
            for copy in tok_send:
                copy.wait_send()
            og_send = [
                remote(og.at[i], ogin.at[z // 2], og_s.at[i], og_r.at[z // 2], at["hosts"][i])
                for i in (0, 1)
            ]
            for copy in og_send:
                copy.start()
        normed, _ = norm_stats(tokin[s].astype(F32))
        n1[s] = (normed * row(gain) + row(shift)).astype(BF)

        @pl.loop(0, blocks)
        def _(c):
            for which, store, scale in ((1, kn, None), (2, vn, None), (0, qn, LOG2E / HEAD**0.5)):
                col = pl.ds(pl.multiple_of(which * width + c * 256, 256), 256)
                made = dot(n1[s], wf[:, col]) + qkv_bias[col].astype(F32).reshape(1, 256)
                if scale is not None:
                    made = made * scale
                made = made.astype(BF)
                for t in (0, 1):
                    store[2 * c + t, s] = made[:, t * PAIR : (t + 1) * PAIR]
                if which == 2:
                    for copy in exchange(s, c):
                        copy.start()

    outer_f = outer.astype(F32)
    inner_f = 1.0 - outer_f
    ones = jnp.ones((16, span), BF)
    key_at = (0, 1, 0, 2, 2 + outer)
    query_at = (0, 1, 1, outer, 1)

    def save_e(hp):
        slot = lax.rem(hp, 2)
        return pltpu.make_async_copy(ee.at[slot], e_h.at[hp], e_sem.at[slot])

    def load_e(hp):
        slot = lax.rem(hp, 2)
        return pltpu.make_async_copy(e_h.at[hp], ee.at[slot], e_sem.at[slot])

    @pl.loop(0, blocks)
    def _(c):
        for s in (0, 1):
            for copy in exchange(s, c):
                copy.wait()

    @pl.loop(0, pairs_n)
    def _(hp):
        slot = lax.rem(hp, 2)

        @pl.when(hp >= 2)
        def _():
            save_e(hp - 2).wait()

        for s in (0, 1):
            q_t = qn[hp, s].T
            for head in (0, 1):
                qp[head, s] = half_rows(q_t, head)
        for kb in range(4):
            vt[kb] = vn[hp, kb].T
        tops = []
        for head in (0, 1):
            tops.append([])
            for j in range(5):
                s_j = dot(kn[hp, key_at[j]], qp[head, query_at[j]]) + bias[j]
                sc[head, j] = s_j
                tops[head].append(jnp.max(s_j, 0, keepdims=True))
        for head in (0, 1):
            m0, m1, m2, m3, m4 = tops[head]
            top_low = jnp.maximum(m0, m3 * inner_f + NEG * outer_f)
            top_high = jnp.maximum(
                jnp.maximum(m1, m2), jnp.maximum(m4, m3 * outer_f + NEG * inner_f)
            )
            top_x = top_high * outer_f + top_low * inner_f
            mixed = []
            for j, top in enumerate((top_low, top_high, top_high, top_x, top_high)):
                e_j = jnp.exp2(sc[head, j] - top).astype(BF)
                ee[slot, j, :, head * span : (head + 1) * span] = e_j
                v_j = jnp.concatenate(
                    [vt[key_at[j], HEAD * head : HEAD * head + HEAD], ones], 0
                )
                mixed.append(dot(v_j, e_j))
            sums = (
                mixed[0] + mixed[3] * inner_f,
                mixed[1] + mixed[2] + mixed[4] + mixed[3] * outer_f,
            )
            for s in (0, 1):
                inv = 1.0 / sums[s][HEAD : HEAD + 1]
                rl[hp, 2 * head + s : 2 * head + s + 1, :] = inv
                ot[hp, s, HEAD * head : HEAD * head + HEAD, :] = (sums[s][:HEAD] * inv).astype(BF)
        for s in (0, 1):
            on[s, :, pl.ds(pl.multiple_of(hp * PAIR, PAIR), PAIR)] = ot[hp, s].T
        save_e(hp).start()

    load_o.wait()
    for s in (0, 1):
        here = pl.ds(s * span, span)
        r = tokin[s].astype(F32) + (dot(on[s], wo[...]) + row(out_bias))
        resid[here] = r
        normed, _ = norm_stats(r)
        n2[here] = (normed * row(gain2) + row(shift2)).astype(BF)
        acc[here] = r + row(proj_bias)

    @pl.loop(0, chunks)
    def _(c):
        slot = lax.rem(c, 2)
        for copy in load_mlp(c):
            copy.wait()
        part_b = fc_bias[pl.ds(pl.multiple_of(c * chunk, chunk), chunk)]
        x = dot(n2[...], fcb[slot]) + part_b.astype(F32).reshape(1, chunk)
        sq = x * x
        half = 0.5 * jnp.tanh(x * ((GELU * 0.044715) * sq + GELU)) + 0.5
        act = x * half
        rise = half + (act - act * half) * ((6.0 * GELU * 0.044715) * sq + 2.0 * GELU)
        slope[c] = rise.astype(BF)
        acc[...] += dot(act.astype(BF), pjb[slot])

        @pl.when(c + 2 < chunks)
        def _():
            for copy in load_mlp(c + 2):
                copy.start()

    for s in (0, 1):
        outst[s] = acc[pl.ds(s * span, span)].astype(BF)
    for i in (0, 1):
        og_send[i].wait_send()
    out_send = [
        remote(
            outst.at[i], out_o.at[lax.rem(z, 2)], out_s.at[i], out_r.at[lax.rem(z, 2)], at["homes"][i]
        )
        for i in (0, 1)
    ]
    for copy in out_send:
        copy.start()
    acc[...] = jnp.zeros_like(acc)
    for hp in (pairs_n - 2, pairs_n - 1):
        save_e(hp).wait()
    for i in (0, 1):
        remote(ogin.at[i], ogin.at[i], og_s.at[i], og_r.at[i], mate).wait_recv()

    @pl.loop(0, chunks)
    def _(t):
        c = chunks - 1 - t
        slot = lax.rem(c, 2)

        @pl.when(t >= 2)
        def _():
            for copy in load_mlp(c):
                copy.wait()

        og_flat = ogin[...].reshape(2 * span, width)
        gh = (dot(og_flat, pjb[slot], NT) * slope[c].astype(F32)).astype(BF)
        acc[...] += dot(gh, fcb[slot], NT)

        @pl.when(c >= 2)
        def _():
            for copy in load_mlp(c - 2):
                copy.start()

    for s in (0, 1):
        here = pl.ds(s * span, span)
        normed, inverse = norm_stats(resid[here])
        g = ogin[s].astype(F32) + norm_back(acc[here], normed, inverse, row(gain2))
        resid[here] = g
        n2[here] = dot(g.astype(BF), wo[...], NT).astype(BF)

    def part_send(hp):
        return remote(part.at[hp], part_in.at[hp], px_s.at[hp], px_r.at[hp], mate)

    @pl.loop(0, pairs_n)
    def _(turn):
        hp = pairs_n - 1 - turn
        slot = lax.rem(hp, 2)
        lanes = pl.ds(pl.multiple_of(hp * PAIR, PAIR), PAIR)

        @pl.when(turn >= 2)
        def _():
            load_e(hp).wait()

        delta = [[None, None], [None, None]]
        for s in (0, 1):
            da_t = n2[s * span : (s + 1) * span, lanes].astype(F32).T
            prod = da_t * ot[hp, s].astype(F32)
            scaled = []
            for head in (0, 1):
                rows_h = slice(HEAD * head, HEAD * head + HEAD)
                inv = rl[hp, 2 * head + s : 2 * head + s + 1, :]
                delta[head][s] = jnp.sum(prod[rows_h], 0, keepdims=True) * inv
                scaled.append(da_t[rows_h] * inv)
            scaled = jnp.concatenate(scaled, 0).astype(BF)
            natural = scaled.T
            q_n = qn[hp, s]
            for head in (0, 1):
                cols = slice(head * span, (head + 1) * span)
                dopc[s, :, cols] = half_rows(scaled, head)
                don[s, cols] = half_lanes(natural, head)
                qm[s, cols] = half_lanes(q_n, head)
        for kb in range(4):
            vt[kb] = kn[hp, kb].T
        for j in range(5):
            for head in (0, 1):
                cols = slice(head * span, (head + 1) * span)
                d_low, d_high = delta[head]
                d_j = (d_low, d_high, d_high, d_high * outer_f + d_low * inner_f, d_high)[j]
                dp = dot(vn[hp, key_at[j]], dopc[query_at[j], :, cols])
                dss[j, :, cols] = (ee[slot, j, :, cols].astype(F32) * (dp - d_j)).astype(BF)
        dk_parts, dv_parts, grads = [], [], [[], []]
        for j in range(5):
            dv_parts.append(dot(ee[slot, j], don[query_at[j]]))
        for j in range(5):
            for head in (0, 1):
                cols = slice(head * span, (head + 1) * span)
                grads[head].append(
                    dot(vt[key_at[j], HEAD * head : HEAD * head + HEAD], dss[j, :, cols])
                )
            dk_parts.append(dot(dss[j], qm[query_at[j]]))
        for t, parts, scale in ((0, dk_parts, LN2), (1, dv_parts, 1.0)):
            store = (dk, dv)[t]
            store[0, :, lanes] = ((parts[0] + parts[2]) * scale).astype(BF)
            store[1, :, lanes] = (parts[1] * scale).astype(BF)
            part[hp, t, 0] = ((parts[3] + parts[4] * inner_f) * scale).astype(BF)
            part[hp, t, 1] = (parts[4] * (outer_f * scale)).astype(BF)
        part_send(hp).start()
        for s in (0, 1):
            rows_t = []
            for head in (0, 1):
                g = grads[head]
                if s == 0:
                    total = g[0] + g[3] * inner_f
                else:
                    total = g[1] + g[2] + g[4] + g[3] * outer_f
                rows_t.append(total * (1.0 / HEAD**0.5))
            on[s, :, lanes] = jnp.concatenate(rows_t, 0).astype(BF).T

        @pl.when(hp >= 2)
        def _():
            load_e(hp - 2).start()

    dq = on

    @pl.loop(0, pairs_n)
    def _(turn):
        hp = pairs_n - 1 - turn
        lanes = pl.ds(pl.multiple_of(hp * PAIR, PAIR), PAIR)
        part_send(hp).wait()
        for t, store in ((0, dk), (1, dv)):
            for s in (0, 1):
                own = store[s, :, lanes].astype(F32)
                store[s, :, lanes] = (own + part_in[hp, t, s].astype(F32)).astype(BF)

    tg_send = []

    def ar_round(r):
        return remote(ar, ar_in.at[r], ar_s.at[r], ar_r.at[r], peers[r])

    for turn in (0, 1):
        s = 1 - z // 2 if turn == 0 else z // 2

        @pl.loop(0, blocks)
        def _(c):
            here = pl.ds(pl.multiple_of(c * 256, 256), 256)
            total = dot(dq[s], wf[here, 0:width], NT)
            total += dot(dk[s], wf[here, width : 2 * width], NT)
            total += dot(dv[s], wf[here, 2 * width : 3 * width], NT)
            acc[0:span, here] = total

        normed, inverse = norm_stats(tokin[s].astype(F32))
        rows_s = pl.ds(pl.multiple_of(s * span, span), span)
        tg[s] = (resid[rows_s] + norm_back(acc[0:span], normed, inverse, row(gain))).astype(BF)
        if turn == 0:
            for i in (0, 1):
                out_send[i].wait_send()
        home = (batch - core + z // 2, low + s * (high - low))
        copy = remote(tg.at[s], tg_o.at[lax.rem(z, 2)], tg_s.at[s], tg_r.at[lax.rem(z, 2)], home)
        copy.start()
        tg_send.append(copy)
        if turn == 0:
            ar[...] = jnp.zeros_like(ar)
            for k, (grad, down, up) in enumerate(((dq, down_q, up_q), (dv, down_v, up_v))):
                up_total = down_total = 0.0
                for i in (0, 1):
                    inner = dot(n1[i], down[...], NT).astype(BF)
                    lift = dot(grad[i], up[...], NT).astype(BF)
                    up_total = up_total + dot(inner, grad[i], TN)
                    down_total = down_total + dot(lift, n1[i], TN)
                ar[2 * k, 0:4] = ADAPTER * up_total
                ar[2 * k + 1, 0:4] = ADAPTER * down_total
            ar_round(0).start()

    for r in range(len(peers)):
        if r > 0:
            ar_round(r).start()
        ar_round(r).wait()
        ar[...] += ar_in[r]
    sums_o[...] = ar[...]

    for i in (0, 1):
        remote(out_o.at[i], out_o.at[i], out_s.at[i], out_r.at[i], mate).wait_recv()
        tg_send[i].wait_send()
        remote(tg_o.at[i], tg_o.at[i], tg_s.at[i], tg_r.at[i], mate).wait_recv()


def deliver_kernel(out_i, tg_i, sums, out_o, tg_o, down_q, up_q, down_v, up_v):
    out_o[...] = out_i[...]
    tg_o[...] = tg_i[...]
    for k, ref in enumerate((up_q, down_q, up_v, down_v)):
        ref[...] = sums[k, 0:4]


VMEM = pl.BlockSpec(memory_space=pltpu.VMEM)
ANY = pl.BlockSpec(memory_space=pl.ANY)
DMA = pltpu.SemaphoreType.DMA
LIMIT = 60 * 1024 * 1024
GELU = 0.7978845608028654


def on_device(
    tokens, doc_starts, attn_gain, attn_shift, qkv_weight, qkv_bias,
    query_down_factor, query_up_factor, value_down_factor, value_up_factor,
    out_weight, out_bias, mlp_gain, mlp_shift, fc_weight, fc_bias, proj_weight, proj_bias, out_grad,
):
    slots, span, width = tokens.shape
    hidden = fc_weight.shape[1]
    rank = query_down_factor.shape[1]
    pairs_n = width // PAIR
    chunk = 1024
    blocks = width // 256
    shape = jax.ShapeDtypeStruct
    two = (slots, span, width)
    flat = (2 * span, width)
    q_shape = (pairs_n, 2, span, PAIR)
    k_shape = (pairs_n, 4, span, PAIR)
    rounds = []
    for axis, size in ((0, lax.axis_size("batch")), (1, lax.axis_size("blk"))):
        distance = 1
        while distance < size:
            rounds.append((axis, distance))
            distance *= 2
    n_rounds = len(rounds)

    def fused(*refs):
        fused_kernel(rounds, *refs)

    bf = lambda *dims: pltpu.VMEM(dims, BF)
    f32 = lambda *dims: pltpu.VMEM(dims, F32)
    out_l, tg_l, sums, _ = pl.pallas_call(
        fused,
        out_shape=(
            shape(two, BF), shape(two, BF), shape((4, 8, width), F32),
            shape((pairs_n, 5, span, 2 * span), BF),
        ),
        in_specs=[ANY] * 6 + [VMEM] * 13,
        out_specs=(ANY, ANY, VMEM, ANY),
        scratch_shapes=[
            bf(*two), bf(*two), bf(width, 3 * width), bf(width, width),
            bf(2, width, chunk), bf(2, chunk, width), bf(*two), bf(*flat),
            bf(*q_shape), bf(*k_shape), bf(*k_shape),
            bf(2, 2, PAIR, span), bf(4, PAIR, span),
            f32(2, 5, span, span), bf(2, 5, span, 2 * span), f32(5, span, span),
            bf(pairs_n, 2, PAIR, span), bf(*two), f32(pairs_n, 8, span),
            f32(*flat), f32(*flat), bf(hidden // chunk, 2 * span, chunk), bf(*two),
            bf(*two), bf(*two),
            bf(2, PAIR, 2 * span), bf(2, 2 * span, PAIR), bf(2, 2 * span, PAIR), bf(5, span, 2 * span),
            bf(pairs_n, 2, 2, span, PAIR), bf(pairs_n, 2, 2, span, PAIR), bf(*two),
            f32(4, 8, width), f32(n_rounds, 4, 8, width), pltpu.VMEM(doc_starts.shape, jnp.int32),
            DMA((2,)), DMA((2,)), DMA((2,)), DMA((2,)),
            DMA((2, blocks, 2)), DMA((2, blocks, 2)), DMA((2,)), DMA((1,)), DMA((2,)), DMA((2,)), DMA((2,)),
            DMA((2,)), DMA((2,)), DMA((2,)), DMA((2,)),
            DMA((pairs_n,)), DMA((pairs_n,)), DMA((n_rounds,)), DMA((n_rounds,)),
        ],
        compiler_params=pltpu.CompilerParams(
            collective_id=0, has_side_effects=True, vmem_limit_bytes=LIMIT
        ),
    )(
        tokens, out_grad, qkv_weight, out_weight, fc_weight, proj_weight, doc_starts,
        attn_gain, attn_shift, qkv_bias, out_bias, mlp_gain, mlp_shift, fc_bias, proj_bias,
        query_down_factor.T, query_up_factor, value_down_factor.T, value_up_factor,
    )

    small = shape((rank, width), F32)
    block = pl.BlockSpec((1, span, width), lambda i: (i, 0, 0))
    whole = lambda *dims: pl.BlockSpec(dims, lambda i: (0,) * len(dims))
    out, tg, down_q, up_q, down_v, up_v = pl.pallas_call(
        deliver_kernel,
        grid=(slots,),
        out_shape=(shape(two, BF), shape(two, BF), small, small, small, small),
        in_specs=[block, block, whole(4, 8, width)],
        out_specs=(block, block) + (whole(rank, width),) * 4,
    )(out_l, tg_l, sums)
    return out, tg, down_q.T, up_q, down_v.T, up_v


def solution(mesh):
    rows = P("batch", "blk", None)
    return jax.shard_map(
        on_device,
        mesh=mesh,
        in_specs=(rows, P("batch", None)) + (P(),) * 16 + (rows,),
        out_specs=(rows, rows, P(), P(), P(), P()),
        check_vma=False,
    )
```

time: 163 us -> 133 us (0.82)
  Pallas kernels: 148 us -> 132 us
  local copies, waits for them, and re-layouts: 14 us -> 0 us
    pallas_call x3 -> x2, Pallas kernels: 148 us -> 132 us  [the longest x1 130 us: on_device(): pl.pallas_call(fused, out_shape=(shape(two, BF), shape(two, BF), shape((4...]
    unnamed x6 -> x0, local copies, waits for them, and re-layouts: 10.3 us -> none
    pallas_call x2 -> x0, local copies, waits for them, and re-layouts: 3.67 us -> none  [on_device(): pl.pallas_call(back, out_shape=(rows_two, rows_two, small(width, rank), s...]
where the time goes in v2:
time: 133 us
  Pallas kernels  132 us (99%)
    pallas_call x1, Pallas kernels, on_device(): pl.pallas_call(fused, out_shape=(shape(two, BF), shape(two, BF), shape((4...  130 us

profile of v2, /device:TPU:0, one launch (start us, length us, event | category | flops | bytes accessed | tf_op | source)
XLA Modules:
  0.0 133.1 jit_solution(4813980852513318263)
XLA Ops:
  0.6 129.6 %shard_map.226 = (bf16[2,256,1024]{2,1,0:T(8,128)(2,1)}, bf16[2,256,1024]{2,1,0:T(8,128)(2,1)}, f32[4,8,1024]{2,1,0:T(8,128)}, bf16[8,5,256,512]{3,2,1,0:T(8,128)(2,1)}) custom-call(bf16[2,256,1024]{2,1,0:T(8,128)(2,1)} %refs_0_.1, bf16[2,256,1024]{2,1,0:T(8,128)(2,1)} %refs_1_.1, bf16[1024,3072]{1,0:T(8,128)(2,1)} %refs_2_.1, bf16[1024,1024]{1,0:T(8,128)(2,1)} %refs_3_.1, ...), custom_call_target="tpu_custom_call" | custom-call | tf_op jit(solution)/shard_map/pallas_call | solution.py:529
  130.3 2.6 %shard_map.227 = (bf16[2,256,1024]{2,1,0:T(8,128)(2,1)}, bf16[2,256,1024]{2,1,0:T(8,128)(2,1)}, f32[4,1024]{1,0:T(4,128)}, f32[4,1024]{1,0:T(4,128)}, f32[4,1024]{1,0:T(4,128)}, /*index=5*/f32[4,1024]{1,0:T(4,128)}) custom-call(bf16[2,256,1024]{2,1,0:T(8,128)(2,1)} %get-tuple-element.15.out_i, bf16[2,256,1024]{2,1,0:T(8,128)(2,1)} %get-tuple-element.16.tg_i, ...), custom_call_target="tpu_custom_call" | custom-call | tf_op jit(solution)/shard_map/pallas_call | solution.py:566

commit v3 on v2

--- a/solution.py
+++ b/solution.py
@@ -105,9 +105,9 @@
     fc_bias, proj_bias, down_q, up_q, down_v, up_v,
     out_o, tg_o, sums_o, e_h,
     tokin, ogin, wf, wo, fcb, pjb, n1, n2, qn, kn, vn, qp, vt, sc, ee, bias, ot, on, rl,
-    resid, acc, slope, outst, dk, dv, dopc, don, qm, dss, part, part_in, tg, ar, ar_in, starts_in,
+    resid, acc, slope, outst, dk, dv, dopc, don, qm, dss, part, part_in, tg, ar, ar_in, z_all, total, starts_in,
     tok_s, tok_r, og_s, og_r, ex_s, ex_r, st_sem, w_sem, fc_sem, pj_sem, e_sem,
-    out_s, out_r, tg_s, tg_r, px_s, px_r, ar_s, ar_r,
+    out_s, out_r, tg_s, tg_r, px_s, px_r, ar_s, ar_r, z_s, z_r, all_s, all_r, sent,
 ):
     at = places()
     z, core, outer = at["z"], at["core"], at["outer"]
@@ -117,17 +117,16 @@
     blocks = width // 256
     chunks, chunk = slope.shape[0], slope.shape[2]
     peers = []
-    for axis, distance in rounds:
-        if axis == 0:
-            bit = lax.rem(batch // distance, 2)
-            peers.append((batch + distance - 2 * distance * bit, z))
-        else:
-            bit = lax.rem(z // distance, 2)
-            peers.append((batch, z + distance - 2 * distance * bit))
+    for distance in rounds:
+        bit = lax.rem(batch // distance, 2)
+        peers.append((batch + distance - 2 * distance * bit, z))
+    depth = z_all.shape[0]
+    z_peers = [(batch, lax.rem(z + d, depth)) for d in range(1, depth)]
+    beside = (batch, z + 1 - 2 * lax.rem(z, 2))
 
     load_w = pltpu.make_async_copy(wqkv, wf, w_sem.at[0])
     load_w.start()
-    greet(at["hosts"] + at["homes"] + [mate] + peers)
+    greet(at["hosts"] + at["homes"] + [mate] + peers + z_peers)
     tok_send = [
         remote(tok.at[i], tokin.at[z // 2], tok_s.at[i], tok_r.at[z // 2], at["hosts"][i])
         for i in (0, 1)
@@ -148,9 +147,6 @@
     load_w.wait()
     load_o = pltpu.make_async_copy(wo_h, wo, w_sem.at[0])
     load_o.start()
-    for c in (0, 1):
-        for copy in load_mlp(c):
-            copy.start()
     for part_w, down, up in ((0, down_q, up_q), (2, down_v, up_v)):
 
         @pl.loop(0, blocks)
@@ -184,12 +180,17 @@
         if turn == 1:
             for copy in tok_send:
                 copy.wait_send()
+            pl.semaphore_signal(sent, inc=1, device_id=beside, device_id_type=MESH)
+            pl.semaphore_wait(sent, 1)
             og_send = [
                 remote(og.at[i], ogin.at[z // 2], og_s.at[i], og_r.at[z // 2], at["hosts"][i])
                 for i in (0, 1)
             ]
             for copy in og_send:
                 copy.start()
+            for c in (0, 1):
+                for copy in load_mlp(c):
+                    copy.start()
         normed, _ = norm_stats(tokin[s].astype(F32))
         n1[s] = (normed * row(gain) + row(shift)).astype(BF)
 
@@ -258,7 +259,7 @@
             mixed = []
             for j, top in enumerate((top_low, top_high, top_high, top_x, top_high)):
                 e_j = jnp.exp2(sc[head, j] - top).astype(BF)
-                ee[slot, j, :, head * span : (head + 1) * span] = e_j
+                ee[slot, head, j] = e_j
                 v_j = jnp.concatenate(
                     [vt[key_at[j], HEAD * head : HEAD * head + HEAD], ones], 0
                 )
@@ -386,10 +387,11 @@
                 d_low, d_high = delta[head]
                 d_j = (d_low, d_high, d_high, d_high * outer_f + d_low * inner_f, d_high)[j]
                 dp = dot(vn[hp, key_at[j]], dopc[query_at[j], :, cols])
-                dss[j, :, cols] = (ee[slot, j, :, cols].astype(F32) * (dp - d_j)).astype(BF)
+                dss[j, :, cols] = (ee[slot, head, j].astype(F32) * (dp - d_j)).astype(BF)
         dk_parts, dv_parts, grads = [], [], [[], []]
         for j in range(5):
-            dv_parts.append(dot(ee[slot, j], don[query_at[j]]))
+            e_pair = jnp.concatenate([ee[slot, 0, j], ee[slot, 1, j]], 1)
+            dv_parts.append(dot(e_pair, don[query_at[j]]))
         for j in range(5):
             for head in (0, 1):
                 cols = slice(head * span, (head + 1) * span)
@@ -431,14 +433,39 @@
                 own = store[s, :, lanes].astype(F32)
                 store[s, :, lanes] = (own + part_in[hp, t, s].astype(F32)).astype(BF)
 
-    tg_send = []
-
-    def ar_round(r):
+    cross, near = 1 - z // 2, z // 2
+    piece = span // 4
+
+    def tg_copy(s, k):
+        rows_k = pl.ds(k * piece, piece)
+        home = (batch - core + z // 2, low + s * (high - low))
+        return remote(
+            tg.at[s, rows_k], tg_o.at[lax.rem(z, 2), rows_k],
+            tg_s.at[s, k], tg_r.at[lax.rem(z, 2), k], home,
+        )
+
+    pieces = ar.shape[0]
+    group = lax.rem(batch, pieces)
+
+    def batch_round(r):
         return remote(ar, ar_in.at[r], ar_s.at[r], ar_r.at[r], peers[r])
 
-    for turn in (0, 1):
-        s = 1 - z // 2 if turn == 0 else z // 2
-
+    def z_send(d):
+        return remote(ar.at[group], z_all.at[z], z_s.at[d], z_r.at[z], z_peers[d])
+
+    def share_round(r):
+        size = 2**r
+        held = pl.ds(group // size * size, size)
+        return remote(total.at[held], total.at[held], all_s.at[r], all_r.at[r], peers[r])
+
+    def share_wait(r):
+        size = 2**r
+        other = group // size
+        other = other + 1 - 2 * lax.rem(other, 2)
+        held = pl.ds(other * size, size)
+        remote(total.at[held], total.at[held], all_s.at[r], all_r.at[r], peers[r]).wait_recv()
+
+    def project_back(s):
         @pl.loop(0, blocks)
         def _(c):
             here = pl.ds(pl.multiple_of(c * 256, 256), 256)
@@ -450,44 +477,66 @@
         normed, inverse = norm_stats(tokin[s].astype(F32))
         rows_s = pl.ds(pl.multiple_of(s * span, span), span)
         tg[s] = (resid[rows_s] + norm_back(acc[0:span], normed, inverse, row(gain))).astype(BF)
-        if turn == 0:
-            for i in (0, 1):
-                out_send[i].wait_send()
-        home = (batch - core + z // 2, low + s * (high - low))
-        copy = remote(tg.at[s], tg_o.at[lax.rem(z, 2)], tg_s.at[s], tg_r.at[lax.rem(z, 2)], home)
-        copy.start()
-        tg_send.append(copy)
-        if turn == 0:
-            ar[...] = jnp.zeros_like(ar)
-            for k, (grad, down, up) in enumerate(((dq, down_q, up_q), (dv, down_v, up_v))):
-                up_total = down_total = 0.0
-                for i in (0, 1):
-                    inner = dot(n1[i], down[...], NT).astype(BF)
-                    lift = dot(grad[i], up[...], NT).astype(BF)
-                    up_total = up_total + dot(inner, grad[i], TN)
-                    down_total = down_total + dot(lift, n1[i], TN)
-                ar[2 * k, 0:4] = ADAPTER * up_total
-                ar[2 * k + 1, 0:4] = ADAPTER * down_total
-            ar_round(0).start()
-
+
+    project_back(cross)
+    for i in (0, 1):
+        out_send[i].wait_send()
+    for k in (0, 1):
+        tg_copy(cross, k).start()
+    for k, (grad, down, up) in enumerate(((dq, down_q, up_q), (dv, down_v, up_v))):
+        up_total = down_total = 0.0
+        for i in (0, 1):
+            inner = dot(n1[i], down[...], NT).astype(BF)
+            lift = dot(grad[i], up[...], NT).astype(BF)
+            up_total = up_total + dot(inner, grad[i], TN)
+            down_total = down_total + dot(lift, n1[i], TN)
+        for c in range(pieces):
+            lanes = slice(c * PAIR, (c + 1) * PAIR)
+            ar[c, 8 * k : 8 * k + 4] = ADAPTER * up_total[:, lanes]
+            ar[c, 8 * k + 4 : 8 * k + 8] = ADAPTER * down_total[:, lanes]
+    batch_round(0).start()
+    project_back(near)
     for r in range(len(peers)):
         if r > 0:
-            ar_round(r).start()
-        ar_round(r).wait()
+            batch_round(r).start()
+        batch_round(r).wait()
         ar[...] += ar_in[r]
-    sums_o[...] = ar[...]
+    for d in range(depth - 1):
+        z_send(d).start()
+    for k in (2, 3):
+        tg_copy(cross, k).start()
+    for k in range(4):
+        tg_copy(near, k).start()
+    z_all[z] = ar[group]
+    for d in range(depth - 1):
+        z_send(d).wait_send()
+        from_z = lax.rem(z + depth - 1 - d, depth)
+        remote(z_all.at[from_z], z_all.at[from_z], z_s.at[d], z_r.at[from_z], mate).wait_recv()
+    summed = z_all[0]
+    for d in range(1, depth):
+        summed = summed + z_all[d]
+    total[group] = summed
+    for r in range(3):
+        share_round(r).start()
+        share_round(r).wait_send()
+        share_wait(r)
+    sums_o[...] = total[...]
 
     for i in (0, 1):
         remote(out_o.at[i], out_o.at[i], out_s.at[i], out_r.at[i], mate).wait_recv()
-        tg_send[i].wait_send()
-        remote(tg_o.at[i], tg_o.at[i], tg_s.at[i], tg_r.at[i], mate).wait_recv()
+        for k in range(4):
+            tg_copy(i, k).wait_send()
+            landed = tg_o.at[i, pl.ds(k * piece, piece)]
+            remote(landed, landed, tg_s.at[i, k], tg_r.at[i, k], mate).wait_recv()
 
 
 def deliver_kernel(out_i, tg_i, sums, out_o, tg_o, down_q, up_q, down_v, up_v):
     out_o[...] = out_i[...]
     tg_o[...] = tg_i[...]
-    for k, ref in enumerate((up_q, down_q, up_v, down_v)):
-        ref[...] = sums[k, 0:4]
+    for c in range(sums.shape[0]):
+        lanes = slice(c * PAIR, (c + 1) * PAIR)
+        for k, ref in enumerate((up_q, down_q, up_v, down_v)):
+            ref[:, lanes] = sums[c, 4 * k : 4 * k + 4]
 
 
 VMEM = pl.BlockSpec(memory_space=pltpu.VMEM)
@@ -513,12 +562,9 @@
     flat = (2 * span, width)
     q_shape = (pairs_n, 2, span, PAIR)
     k_shape = (pairs_n, 4, span, PAIR)
-    rounds = []
-    for axis, size in ((0, lax.axis_size("batch")), (1, lax.axis_size("blk"))):
-        distance = 1
-        while distance < size:
-            rounds.append((axis, distance))
-            distance *= 2
+    rounds = [2**r for r in range((lax.axis_size("batch") - 1).bit_length())]
+    depth = lax.axis_size("blk")
+    pieces = width // PAIR
     n_rounds = len(rounds)
 
     def fused(*refs):
@@ -529,8 +575,8 @@
     out_l, tg_l, sums, _ = pl.pallas_call(
         fused,
         out_shape=(
-            shape(two, BF), shape(two, BF), shape((4, 8, width), F32),
-            shape((pairs_n, 5, span, 2 * span), BF),
+            shape(two, BF), shape(two, BF), shape((pieces, 16, PAIR), F32),
+            shape((pairs_n, 2, 5, span, span), BF),
         ),
         in_specs=[ANY] * 6 + [VMEM] * 13,
         out_specs=(ANY, ANY, VMEM, ANY),
@@ -539,17 +585,19 @@
             bf(2, width, chunk), bf(2, chunk, width), bf(*two), bf(*flat),
             bf(*q_shape), bf(*k_shape), bf(*k_shape),
             bf(2, 2, PAIR, span), bf(4, PAIR, span),
-            f32(2, 5, span, span), bf(2, 5, span, 2 * span), f32(5, span, span),
+            f32(2, 5, span, span), bf(2, 2, 5, span, span), f32(5, span, span),
             bf(pairs_n, 2, PAIR, span), bf(*two), f32(pairs_n, 8, span),
             f32(*flat), f32(*flat), bf(hidden // chunk, 2 * span, chunk), bf(*two),
             bf(*two), bf(*two),
             bf(2, PAIR, 2 * span), bf(2, 2 * span, PAIR), bf(2, 2 * span, PAIR), bf(5, span, 2 * span),
             bf(pairs_n, 2, 2, span, PAIR), bf(pairs_n, 2, 2, span, PAIR), bf(*two),
-            f32(4, 8, width), f32(n_rounds, 4, 8, width), pltpu.VMEM(doc_starts.shape, jnp.int32),
+            f32(pieces, 16, PAIR), f32(n_rounds, pieces, 16, PAIR), f32(depth, 16, PAIR), f32(pieces, 16, PAIR),
+            pltpu.VMEM(doc_starts.shape, jnp.int32),
             DMA((2,)), DMA((2,)), DMA((2,)), DMA((2,)),
             DMA((2, blocks, 2)), DMA((2, blocks, 2)), DMA((2,)), DMA((1,)), DMA((2,)), DMA((2,)), DMA((2,)),
-            DMA((2,)), DMA((2,)), DMA((2,)), DMA((2,)),
+            DMA((2,)), DMA((2,)), DMA((2, 4)), DMA((2, 4)),
             DMA((pairs_n,)), DMA((pairs_n,)), DMA((n_rounds,)), DMA((n_rounds,)),
+            DMA((depth - 1,)), DMA((depth,)), DMA((3,)), DMA((3,)), pltpu.SemaphoreType.REGULAR,
         ],
         compiler_params=pltpu.CompilerParams(
             collective_id=0, has_side_effects=True, vmem_limit_bytes=LIMIT
@@ -567,7 +615,7 @@
         deliver_kernel,
         grid=(slots,),
         out_shape=(shape(two, BF), shape(two, BF), small, small, small, small),
-        in_specs=[block, block, whole(4, 8, width)],
+        in_specs=[block, block, whole(pieces, 16, PAIR)],
         out_specs=(block, block) + (whole(rank, width),) * 4,
     )(out_l, tg_l, sums)
     return out, tg, down_q.T, up_q, down_v.T, up_v

time: 133 us -> 120 us (0.902)
  Pallas kernels: 132 us -> 119 us
    pallas_call x1, Pallas kernels: 130 us -> 117 us  [on_device(): pl.pallas_call(fused, out_shape=(shape(two, BF), shape(two, BF), shape((p...]
where the time goes in v3:
time: 120 us
  Pallas kernels  119 us (99%)
    pallas_call x1, Pallas kernels, on_device(): pl.pallas_call(fused, out_shape=(shape(two, BF), shape(two, BF), shape((p...  117 us
    pallas_call x1, Pallas kernels, on_device(): pl.pallas_call(deliver_kernel, grid=(slots,), out_shape=(shape(two, BF),...  2.62 us

profile of v3, /device:TPU:0, one launch (start us, length us, event | category | flops | bytes accessed | tf_op | source)
XLA Modules:
  0.0 120.0 jit_solution(4878228483202778402)
XLA Ops:
  0.6 116.5 %shard_map.226 = (bf16[2,256,1024]{2,1,0:T(8,128)(2,1)}, bf16[2,256,1024]{2,1,0:T(8,128)(2,1)}, f32[8,16,128]{2,1,0:T(8,128)}, bf16[8,2,5,256,256]{4,3,2,1,0:T(8,128)(2,1)}) custom-call(bf16[2,256,1024]{2,1,0:T(8,128)(2,1)} %refs_0_.1, bf16[2,256,1024]{2,1,0:T(8,128)(2,1)} %refs_1_.1, bf16[1024,3072]{1,0:T(8,128)(2,1)} %refs_2_.1, ...), custom_call_target="tpu_custom_call" | custom-call | tf_op jit(solution)/shard_map/pallas_call | solution.py:575
  117.2 2.6 %shard_map.227 = (bf16[2,256,1024]{2,1,0:T(8,128)(2,1)}, bf16[2,256,1024]{2,1,0:T(8,128)(2,1)}, f32[4,1024]{1,0:T(4,128)}, f32[4,1024]{1,0:T(4,128)}, f32[4,1024]{1,0:T(4,128)}, /*index=5*/f32[4,1024]{1,0:T(4,128)}) custom-call(bf16[2,256,1024]{2,1,0:T(8,128)(2,1)} %get-tuple-element.15.out_i, bf16[2,256,1024]{2,1,0:T(8,128)(2,1)} %get-tuple-element.16.tg_i, ...), custom_call_target="tpu_custom_call" | custom-call | tf_op jit(solution)/shard_map/pallas_call | solution.py:614

commit v4 on v3

--- a/solution.py
+++ b/solution.py
@@ -105,7 +105,7 @@
     fc_bias, proj_bias, down_q, up_q, down_v, up_v,
     out_o, tg_o, sums_o, e_h,
     tokin, ogin, wf, wo, fcb, pjb, n1, n2, qn, kn, vn, qp, vt, sc, ee, bias, ot, on, rl,
-    resid, acc, slope, outst, dk, dv, dopc, don, qm, dss, part, part_in, tg, ar, ar_in, z_all, total, starts_in,
+    resid, acc, slope, outst, dv, dopc, don, qm, dss, part, part_in, ar, ar_in, z_all, total, starts_in,
     tok_s, tok_r, og_s, og_r, ex_s, ex_r, st_sem, w_sem, fc_sem, pj_sem, e_sem,
     out_s, out_r, tg_s, tg_r, px_s, px_r, ar_s, ar_r, z_s, z_r, all_s, all_r, sent,
 ):
@@ -214,28 +214,18 @@
     key_at = (0, 1, 0, 2, 2 + outer)
     query_at = (0, 1, 1, outer, 1)
 
+    kept = ee.shape[0]
+
     def save_e(hp):
-        slot = lax.rem(hp, 2)
+        slot = lax.rem(hp, kept)
         return pltpu.make_async_copy(ee.at[slot], e_h.at[hp], e_sem.at[slot])
 
     def load_e(hp):
-        slot = lax.rem(hp, 2)
+        slot = lax.rem(hp, kept)
         return pltpu.make_async_copy(e_h.at[hp], ee.at[slot], e_sem.at[slot])
 
-    @pl.loop(0, blocks)
-    def _(c):
-        for s in (0, 1):
-            for copy in exchange(s, c):
-                copy.wait()
-
-    @pl.loop(0, pairs_n)
-    def _(hp):
-        slot = lax.rem(hp, 2)
-
-        @pl.when(hp >= 2)
-        def _():
-            save_e(hp - 2).wait()
-
+    def attend(hp):
+        slot = lax.rem(hp, kept)
         for s in (0, 1):
             q_t = qn[hp, s].T
             for head in (0, 1):
@@ -274,7 +264,23 @@
                 ot[hp, s, HEAD * head : HEAD * head + HEAD, :] = (sums[s][:HEAD] * inv).astype(BF)
         for s in (0, 1):
             on[s, :, pl.ds(pl.multiple_of(hp * PAIR, PAIR), PAIR)] = ot[hp, s].T
-        save_e(hp).start()
+        @pl.when(hp + kept < pairs_n)
+        def _():
+            save_e(hp).start()
+
+    @pl.loop(0, pairs_n // 2)
+    def _(step):
+        for s in (0, 1):
+            for copy in exchange(s, step):
+                copy.wait()
+
+        @pl.when(2 * step >= kept)
+        def _():
+            for t in (0, 1):
+                save_e(2 * step + t - kept).wait()
+
+        for t in (0, 1):
+            attend(2 * step + t)
 
     load_o.wait()
     for s in (0, 1):
@@ -282,7 +288,7 @@
         r = tokin[s].astype(F32) + (dot(on[s], wo[...]) + row(out_bias))
         resid[here] = r
         normed, _ = norm_stats(r)
-        n2[here] = (normed * row(gain2) + row(shift2)).astype(BF)
+        n2[s] = (normed * row(gain2) + row(shift2)).astype(BF)
         acc[here] = r + row(proj_bias)
 
     @pl.loop(0, chunks)
@@ -291,7 +297,7 @@
         for copy in load_mlp(c):
             copy.wait()
         part_b = fc_bias[pl.ds(pl.multiple_of(c * chunk, chunk), chunk)]
-        x = dot(n2[...], fcb[slot]) + part_b.astype(F32).reshape(1, chunk)
+        x = dot(n2[...].reshape(2 * span, width), fcb[slot]) + part_b.astype(F32).reshape(1, chunk)
         sq = x * x
         half = 0.5 * jnp.tanh(x * ((GELU * 0.044715) * sq + GELU)) + 0.5
         act = x * half
@@ -317,8 +323,6 @@
     for copy in out_send:
         copy.start()
     acc[...] = jnp.zeros_like(acc)
-    for hp in (pairs_n - 2, pairs_n - 1):
-        save_e(hp).wait()
     for i in (0, 1):
         remote(ogin.at[i], ogin.at[i], og_s.at[i], og_r.at[i], mate).wait_recv()
 
@@ -346,24 +350,19 @@
         normed, inverse = norm_stats(resid[here])
         g = ogin[s].astype(F32) + norm_back(acc[here], normed, inverse, row(gain2))
         resid[here] = g
-        n2[here] = dot(g.astype(BF), wo[...], NT).astype(BF)
+        n2[s] = dot(g.astype(BF), wo[...], NT).astype(BF)
+
+    dk = ogin
 
     def part_send(hp):
         return remote(part.at[hp], part_in.at[hp], px_s.at[hp], px_r.at[hp], mate)
 
-    @pl.loop(0, pairs_n)
-    def _(turn):
-        hp = pairs_n - 1 - turn
-        slot = lax.rem(hp, 2)
+    def attend_back(hp):
+        slot = lax.rem(hp, kept)
         lanes = pl.ds(pl.multiple_of(hp * PAIR, PAIR), PAIR)
-
-        @pl.when(turn >= 2)
-        def _():
-            load_e(hp).wait()
-
         delta = [[None, None], [None, None]]
         for s in (0, 1):
-            da_t = n2[s * span : (s + 1) * span, lanes].astype(F32).T
+            da_t = n2[s, :, lanes].astype(F32).T
             prod = da_t * ot[hp, s].astype(F32)
             scaled = []
             for head in (0, 1):
@@ -417,9 +416,22 @@
                 rows_t.append(total * (1.0 / HEAD**0.5))
             on[s, :, lanes] = jnp.concatenate(rows_t, 0).astype(BF).T
 
-        @pl.when(hp >= 2)
+    @pl.loop(0, pairs_n // 2)
+    def _(turn):
+        step = pairs_n // 2 - 1 - turn
+
+        @pl.when(2 * step + kept < pairs_n)
         def _():
-            load_e(hp - 2).start()
+            for t in (0, 1):
+                load_e(2 * step + t).wait()
+
+        for t in (1, 0):
+            attend_back(2 * step + t)
+
+        @pl.when(2 * step >= kept)
+        def _():
+            for t in (0, 1):
+                load_e(2 * step + t - kept).start()
 
     dq = on
 
@@ -435,6 +447,7 @@
 
     cross, near = 1 - z // 2, z // 2
     piece = span // 4
+    tg = n2
 
     def tg_copy(s, k):
         rows_k = pl.ds(k * piece, piece)
@@ -503,10 +516,10 @@
         ar[...] += ar_in[r]
     for d in range(depth - 1):
         z_send(d).start()
+    for k in range(4):
+        tg_copy(near, k).start()
     for k in (2, 3):
         tg_copy(cross, k).start()
-    for k in range(4):
-        tg_copy(near, k).start()
     z_all[z] = ar[group]
     for d in range(depth - 1):
         z_send(d).wait_send()
@@ -576,25 +589,25 @@
         fused,
         out_shape=(
             shape(two, BF), shape(two, BF), shape((pieces, 16, PAIR), F32),
-            shape((pairs_n, 2, 5, span, span), BF),
+            shape((max(pairs_n - 4, 1), 2, 5, span, span), BF),
         ),
         in_specs=[ANY] * 6 + [VMEM] * 13,
         out_specs=(ANY, ANY, VMEM, ANY),
         scratch_shapes=[
             bf(*two), bf(*two), bf(width, 3 * width), bf(width, width),
-            bf(2, width, chunk), bf(2, chunk, width), bf(*two), bf(*flat),
+            bf(2, width, chunk), bf(2, chunk, width), bf(*two), bf(*two),
             bf(*q_shape), bf(*k_shape), bf(*k_shape),
             bf(2, 2, PAIR, span), bf(4, PAIR, span),
-            f32(2, 5, span, span), bf(2, 2, 5, span, span), f32(5, span, span),
+            f32(2, 5, span, span), bf(4, 2, 5, span, span), f32(5, span, span),
             bf(pairs_n, 2, PAIR, span), bf(*two), f32(pairs_n, 8, span),
             f32(*flat), f32(*flat), bf(hidden // chunk, 2 * span, chunk), bf(*two),
-            bf(*two), bf(*two),
+            bf(*two),
             bf(2, PAIR, 2 * span), bf(2, 2 * span, PAIR), bf(2, 2 * span, PAIR), bf(5, span, 2 * span),
-            bf(pairs_n, 2, 2, span, PAIR), bf(pairs_n, 2, 2, span, PAIR), bf(*two),
+            bf(pairs_n, 2, 2, span, PAIR), bf(pairs_n, 2, 2, span, PAIR),
             f32(pieces, 16, PAIR), f32(n_rounds, pieces, 16, PAIR), f32(depth, 16, PAIR), f32(pieces, 16, PAIR),
             pltpu.VMEM(doc_starts.shape, jnp.int32),
             DMA((2,)), DMA((2,)), DMA((2,)), DMA((2,)),
-            DMA((2, blocks, 2)), DMA((2, blocks, 2)), DMA((2,)), DMA((1,)), DMA((2,)), DMA((2,)), DMA((2,)),
+            DMA((2, blocks, 2)), DMA((2, blocks, 2)), DMA((2,)), DMA((1,)), DMA((2,)), DMA((2,)), DMA((4,)),
             DMA((2,)), DMA((2,)), DMA((2, 4)), DMA((2, 4)),
             DMA((pairs_n,)), DMA((pairs_n,)), DMA((n_rounds,)), DMA((n_rounds,)),
             DMA((depth - 1,)), DMA((depth,)), DMA((3,)), DMA((3,)), pltpu.SemaphoreType.REGULAR,

time: 120 us -> 116 us (0.967)
  Pallas kernels: 119 us -> 115 us
    pallas_call x1, Pallas kernels: 117 us -> 112 us  [on_device(): pl.pallas_call(fused, out_shape=(shape(two, BF), shape(two, BF), shape((p...]
where the time goes in v4:
time: 116 us; the launch traced here: 115 us
  Pallas kernels  115 us (99%)
    pallas_call x1, Pallas kernels, on_device(): pl.pallas_call(fused, out_shape=(shape(two, BF), shape(two, BF), shape((p...  112 us
    pallas_call x1, Pallas kernels, on_device(): pl.pallas_call(deliver_kernel, grid=(slots,), out_shape=(shape(two, BF),...  2.62 us

profile of v4, /device:TPU:0, one launch (start us, length us, event | category | flops | bytes accessed | tf_op | source)
XLA Modules:
  0.0 115.3 jit_solution(12996993288951715532)
XLA Ops:
  0.6 111.9 %shard_map.226 = (bf16[2,256,1024]{2,1,0:T(8,128)(2,1)}, bf16[2,256,1024]{2,1,0:T(8,128)(2,1)}, f32[8,16,128]{2,1,0:T(8,128)}, bf16[4,2,5,256,256]{4,3,2,1,0:T(8,128)(2,1)}) custom-call(bf16[2,256,1024]{2,1,0:T(8,128)(2,1)} %refs_0_.1, bf16[2,256,1024]{2,1,0:T(8,128)(2,1)} %refs_1_.1, bf16[1024,3072]{1,0:T(8,128)(2,1)} %refs_2_.1, ...), custom_call_target="tpu_custom_call" | custom-call | tf_op jit(solution)/shard_map/pallas_call | solution.py:588
  112.5 2.6 %shard_map.227 = (bf16[2,256,1024]{2,1,0:T(8,128)(2,1)}, bf16[2,256,1024]{2,1,0:T(8,128)(2,1)}, f32[4,1024]{1,0:T(4,128)}, f32[4,1024]{1,0:T(4,128)}, f32[4,1024]{1,0:T(4,128)}, /*index=5*/f32[4,1024]{1,0:T(4,128)}) custom-call(bf16[2,256,1024]{2,1,0:T(8,128)(2,1)} %get-tuple-element.15.out_i, bf16[2,256,1024]{2,1,0:T(8,128)(2,1)} %get-tuple-element.16.tg_i, ...), custom_call_target="tpu_custom_call" | custom-call | tf_op jit(solution)/shard_map/pallas_call | solution.py:627

commit v5 on v4

--- a/solution.py
+++ b/solution.py
@@ -101,14 +101,17 @@
 
 def fused_kernel(
     rounds,
-    tok, og, wqkv, wo_h, fc_h, proj_h, starts, gain, shift, qkv_bias, out_bias, gain2, shift2,
-    fc_bias, proj_bias, down_q, up_q, down_v, up_v,
-    out_o, tg_o, sums_o, e_h,
-    tokin, ogin, wf, wo, fcb, pjb, n1, n2, qn, kn, vn, qp, vt, sc, ee, bias, ot, on, rl,
-    resid, acc, slope, outst, dv, dopc, don, qm, dss, part, part_in, ar, ar_in, z_all, total, starts_in,
-    tok_s, tok_r, og_s, og_r, ex_s, ex_r, st_sem, w_sem, fc_sem, pj_sem, e_sem,
-    out_s, out_r, tg_s, tg_r, px_s, px_r, ar_s, ar_r, z_s, z_r, all_s, all_r, sent,
+    tok, og, wqkv, wo_h, fc_h, proj_h, *rest,
 ):
+    (
+        starts_h, gain_h, shift_h, qkv_bias_h, out_bias_h, gain2_h, shift2_h, fc_bias_h, proj_bias_h, down_q_h, up_q_h, down_v_h, up_v_h,
+        out_o, tg_o, sums_o, e_h,
+        tokin, ogin, wf, wo, fcb, pjb, n1, n2, qn, kn, vn, qp, vt, sc, ee, bias, ot, on, rl,
+        resid, acc, slope, outst, dv, dopc, don, qm, dss, part, part_in, ar, ar_in, piece_sum, far_in, z_all, total, starts_in,
+        tok_s, tok_r, og_s, og_r, ex_s, ex_r, st_sem, w_sem, fc_sem, pj_sem, e_sem,
+        out_s, out_r, tg_s, tg_r, px_s, px_r, ar_s, ar_r, far_s, far_r, z_s, z_r, all_s, all_r, sent,
+        starts, gain, shift, qkv_bias, out_bias, gain2, shift2, fc_bias, proj_bias, down_q, up_q, down_v, up_v, small_sem,
+    ) = rest
     at = places()
     z, core, outer = at["z"], at["core"], at["outer"]
     low, high, mate, batch = at["low"], at["high"], at["mate"], at["batch"]
@@ -116,23 +119,38 @@
     pairs_n = qn.shape[0]
     blocks = width // 256
     chunks, chunk = slope.shape[0], slope.shape[2]
-    peers = []
+    pieces = ar.shape[0]
+    group = lax.rem(batch, pieces)
+    around = [
+        (batch - group + lax.rem(group + d, pieces), z) for d in range(1, pieces)
+    ]
+    far = []
     for distance in rounds:
         bit = lax.rem(batch // distance, 2)
-        peers.append((batch + distance - 2 * distance * bit, z))
+        far.append((batch + distance - 2 * distance * bit, z))
     depth = z_all.shape[0]
     z_peers = [(batch, lax.rem(z + d, depth)) for d in range(1, depth)]
     beside = (batch, z + 1 - 2 * lax.rem(z, 2))
 
     load_w = pltpu.make_async_copy(wqkv, wf, w_sem.at[0])
     load_w.start()
-    greet(at["hosts"] + at["homes"] + [mate] + peers + z_peers)
+    greet(at["hosts"] + at["homes"] + [mate] + around + far + z_peers)
     tok_send = [
         remote(tok.at[i], tokin.at[z // 2], tok_s.at[i], tok_r.at[z // 2], at["hosts"][i])
         for i in (0, 1)
     ]
     for copy in tok_send:
         copy.start()
+    small = [
+        pltpu.make_async_copy(src, dst, small_sem.at[k])
+        for k, (src, dst) in enumerate((
+            (starts_h, starts), (gain_h, gain), (shift_h, shift), (qkv_bias_h, qkv_bias), (out_bias_h, out_bias), (gain2_h, gain2), (shift2_h, shift2), (fc_bias_h, fc_bias), (proj_bias_h, proj_bias), (down_q_h, down_q), (up_q_h, up_q), (down_v_h, down_v), (up_v_h, up_v),
+        ))
+    ]
+    for copy in small:
+        copy.start()
+    for copy in small:
+        copy.wait()
     starts_copy = remote(starts, starts_in, st_sem.at[0], st_sem.at[1], mate)
     starts_copy.start()
 
@@ -176,11 +194,12 @@
 
     for turn in (0, 1):
         s = z // 2 if turn == 0 else 1 - z // 2
-        remote(tokin.at[s], tokin.at[s], tok_s.at[0], tok_r.at[s], mate).wait_recv()
         if turn == 1:
             for copy in tok_send:
                 copy.wait_send()
             pl.semaphore_signal(sent, inc=1, device_id=beside, device_id_type=MESH)
+        remote(tokin.at[s], tokin.at[s], tok_s.at[0], tok_r.at[s], mate).wait_recv()
+        if turn == 1:
             pl.semaphore_wait(sent, 1)
             og_send = [
                 remote(og.at[i], ogin.at[z // 2], og_s.at[i], og_r.at[z // 2], at["hosts"][i])
@@ -457,45 +476,58 @@
             tg_s.at[s, k], tg_r.at[lax.rem(z, 2), k], home,
         )
 
-    pieces = ar.shape[0]
-    group = lax.rem(batch, pieces)
-
-    def batch_round(r):
-        return remote(ar, ar_in.at[r], ar_s.at[r], ar_r.at[r], peers[r])
+    def spread(d):
+        there = lax.rem(group + d, pieces)
+        return remote(
+            ar.at[there], ar_in.at[group], ar_s.at[d - 1], ar_r.at[group], around[d - 1]
+        )
+
+    def spread_wait(d):
+        sender = lax.rem(group + pieces - d, pieces)
+        spread(d).wait_send()
+        remote(
+            ar_in.at[sender], ar_in.at[sender], ar_s.at[d - 1], ar_r.at[sender], mate
+        ).wait_recv()
+
+    def far_round(r):
+        return remote(piece_sum, far_in.at[r], far_s.at[r], far_r.at[r], far[r])
 
     def z_send(d):
-        return remote(ar.at[group], z_all.at[z], z_s.at[d], z_r.at[z], z_peers[d])
-
-    def share_round(r):
-        size = 2**r
-        held = pl.ds(group // size * size, size)
-        return remote(total.at[held], total.at[held], all_s.at[r], all_r.at[r], peers[r])
-
-    def share_wait(r):
-        size = 2**r
-        other = group // size
-        other = other + 1 - 2 * lax.rem(other, 2)
-        held = pl.ds(other * size, size)
-        remote(total.at[held], total.at[held], all_s.at[r], all_r.at[r], peers[r]).wait_recv()
-
-    def project_back(s):
+        return remote(piece_sum, z_all.at[z], z_s.at[d], z_r.at[z], z_peers[d])
+
+    def share(d):
+        return remote(
+            total.at[group], total.at[group], all_s.at[d - 1], all_r.at[group], around[d - 1]
+        )
+
+    def share_wait(d):
+        sender = lax.rem(group + pieces - d, pieces)
+        share(d).wait_send()
+        remote(
+            total.at[sender], total.at[sender], all_s.at[d - 1], all_r.at[sender], mate
+        ).wait_recv()
+
+    def project_back(s, first, count):
+        rows_p = slice(first, first + count)
+
         @pl.loop(0, blocks)
         def _(c):
             here = pl.ds(pl.multiple_of(c * 256, 256), 256)
-            total = dot(dq[s], wf[here, 0:width], NT)
-            total += dot(dk[s], wf[here, width : 2 * width], NT)
-            total += dot(dv[s], wf[here, 2 * width : 3 * width], NT)
-            acc[0:span, here] = total
-
-        normed, inverse = norm_stats(tokin[s].astype(F32))
-        rows_s = pl.ds(pl.multiple_of(s * span, span), span)
-        tg[s] = (resid[rows_s] + norm_back(acc[0:span], normed, inverse, row(gain))).astype(BF)
-
-    project_back(cross)
+            made = dot(dq[s, rows_p], wf[here, 0:width], NT)
+            made += dot(dk[s, rows_p], wf[here, width : 2 * width], NT)
+            made += dot(dv[s, rows_p], wf[here, 2 * width : 3 * width], NT)
+            acc[rows_p, here] = made
+
+        normed, inverse = norm_stats(tokin[s, rows_p].astype(F32))
+        rows_s = pl.ds(pl.multiple_of(s * span + first, count), count)
+        back = norm_back(acc[rows_p], normed, inverse, row(gain))
+        tg[s, rows_p] = (resid[rows_s] + back).astype(BF)
+
+    project_back(cross, 0, span // 2)
     for i in (0, 1):
         out_send[i].wait_send()
-    for k in (0, 1):
-        tg_copy(cross, k).start()
+    tg_copy(cross, 0).start()
+    project_back(cross, span // 2, span // 2)
     for k, (grad, down, up) in enumerate(((dq, down_q, up_q), (dv, down_v, up_v))):
         up_total = down_total = 0.0
         for i in (0, 1):
@@ -507,20 +539,28 @@
             lanes = slice(c * PAIR, (c + 1) * PAIR)
             ar[c, 8 * k : 8 * k + 4] = ADAPTER * up_total[:, lanes]
             ar[c, 8 * k + 4 : 8 * k + 8] = ADAPTER * down_total[:, lanes]
-    batch_round(0).start()
-    project_back(near)
-    for r in range(len(peers)):
-        if r > 0:
-            batch_round(r).start()
-        batch_round(r).wait()
-        ar[...] += ar_in[r]
+    for d in range(1, pieces):
+        spread(d).start()
+    ar_in[group] = ar[group]
+    tg_copy(cross, 1).start()
+    project_back(near, 0, span)
+    for d in range(1, pieces):
+        spread_wait(d)
+    added = ar_in[0]
+    for d in range(1, pieces):
+        added = added + ar_in[d]
+    piece_sum[...] = added
+    for r in range(len(far)):
+        far_round(r).start()
+        far_round(r).wait()
+        piece_sum[...] += far_in[r]
     for d in range(depth - 1):
         z_send(d).start()
     for k in range(4):
         tg_copy(near, k).start()
     for k in (2, 3):
         tg_copy(cross, k).start()
-    z_all[z] = ar[group]
+    z_all[z] = piece_sum[...]
     for d in range(depth - 1):
         z_send(d).wait_send()
         from_z = lax.rem(z + depth - 1 - d, depth)
@@ -529,10 +569,10 @@
     for d in range(1, depth):
         summed = summed + z_all[d]
     total[group] = summed
-    for r in range(3):
-        share_round(r).start()
-        share_round(r).wait_send()
-        share_wait(r)
+    for d in range(1, pieces):
+        share(d).start()
+    for d in range(1, pieces):
+        share_wait(d)
     sums_o[...] = total[...]
 
     for i in (0, 1):
@@ -575,10 +615,12 @@
     flat = (2 * span, width)
     q_shape = (pairs_n, 2, span, PAIR)
     k_shape = (pairs_n, 4, span, PAIR)
-    rounds = [2**r for r in range((lax.axis_size("batch") - 1).bit_length())]
     depth = lax.axis_size("blk")
     pieces = width // PAIR
-    n_rounds = len(rounds)
+    rounds = []
+    while pieces << len(rounds) < lax.axis_size("batch"):
+        rounds.append(pieces << len(rounds))
+    n_rounds = max(len(rounds), 1)
 
     def fused(*refs):
         fused_kernel(rounds, *refs)
@@ -591,7 +633,7 @@
             shape(two, BF), shape(two, BF), shape((pieces, 16, PAIR), F32),
             shape((max(pairs_n - 4, 1), 2, 5, span, span), BF),
         ),
-        in_specs=[ANY] * 6 + [VMEM] * 13,
+        in_specs=[ANY] * 19,
         out_specs=(ANY, ANY, VMEM, ANY),
         scratch_shapes=[
             bf(*two), bf(*two), bf(width, 3 * width), bf(width, width),
@@ -604,13 +646,16 @@
             bf(*two),
             bf(2, PAIR, 2 * span), bf(2, 2 * span, PAIR), bf(2, 2 * span, PAIR), bf(5, span, 2 * span),
             bf(pairs_n, 2, 2, span, PAIR), bf(pairs_n, 2, 2, span, PAIR),
-            f32(pieces, 16, PAIR), f32(n_rounds, pieces, 16, PAIR), f32(depth, 16, PAIR), f32(pieces, 16, PAIR),
+            f32(pieces, 16, PAIR), f32(pieces, 16, PAIR), f32(16, PAIR), f32(n_rounds, 16, PAIR),
+            f32(depth, 16, PAIR), f32(pieces, 16, PAIR),
             pltpu.VMEM(doc_starts.shape, jnp.int32),
             DMA((2,)), DMA((2,)), DMA((2,)), DMA((2,)),
             DMA((2, blocks, 2)), DMA((2, blocks, 2)), DMA((2,)), DMA((1,)), DMA((2,)), DMA((2,)), DMA((4,)),
             DMA((2,)), DMA((2,)), DMA((2, 4)), DMA((2, 4)),
-            DMA((pairs_n,)), DMA((pairs_n,)), DMA((n_rounds,)), DMA((n_rounds,)),
-            DMA((depth - 1,)), DMA((depth,)), DMA((3,)), DMA((3,)), pltpu.SemaphoreType.REGULAR,
+            DMA((pairs_n,)), DMA((pairs_n,)), DMA((pieces - 1,)), DMA((pieces,)), DMA((n_rounds,)), DMA((n_rounds,)),
+            DMA((depth - 1,)), DMA((depth,)), DMA((pieces - 1,)), DMA((pieces,)), pltpu.SemaphoreType.REGULAR,
+            pltpu.VMEM(doc_starts.shape, jnp.int32), bf(width), bf(width), bf(3 * width), bf(width), bf(width), bf(width),
+            bf(hidden), bf(width), bf(rank, width), bf(rank, width), bf(rank, width), bf(rank, width), DMA((13,)),
         ],
         compiler_params=pltpu.CompilerParams(
             collective_id=0, has_side_effects=True, vmem_limit_bytes=LIMIT

time: 116 us -> 113 us (0.974)
  Pallas kernels: 115 us -> 111 us
    pallas_call x1, Pallas kernels: 112 us -> 108 us  [on_device(): pl.pallas_call(fused, out_shape=(shape(two, BF), shape(two, BF), shape((p...]
where the time goes in v5:
time: 113 us; the launch traced here: 111 us
  Pallas kernels  111 us (98%)
    pallas_call x1, Pallas kernels, on_device(): pl.pallas_call(fused, out_shape=(shape(two, BF), shape(two, BF), shape((p...  108 us
    pallas_call x1, Pallas kernels, on_device(): pl.pallas_call(deliver_kernel, grid=(slots,), out_shape=(shape(two, BF),...  2.62 us

profile of v5, /device:TPU:0, one launch (start us, length us, event | category | flops | bytes accessed | tf_op | source)
XLA Modules:
  0.0 111.5 jit_solution(15138442450178113522)
XLA Ops:
  0.6 108.0 %shard_map.226 = (bf16[2,256,1024]{2,1,0:T(8,128)(2,1)}, bf16[2,256,1024]{2,1,0:T(8,128)(2,1)}, f32[8,16,128]{2,1,0:T(8,128)}, bf16[4,2,5,256,256]{4,3,2,1,0:T(8,128)(2,1)}) custom-call(bf16[2,256,1024]{2,1,0:T(8,128)(2,1)} %refs_0_.1, bf16[2,256,1024]{2,1,0:T(8,128)(2,1)} %refs_1_.1, bf16[1024,3072]{1,0:T(8,128)(2,1)} %refs_2_.1, ...), custom_call_target="tpu_custom_call" | custom-call | tf_op jit(solution)/shard_map/pallas_call | solution.py:630
  108.7 2.6 %shard_map.227 = (bf16[2,256,1024]{2,1,0:T(8,128)(2,1)}, bf16[2,256,1024]{2,1,0:T(8,128)(2,1)}, f32[4,1024]{1,0:T(4,128)}, f32[4,1024]{1,0:T(4,128)}, f32[4,1024]{1,0:T(4,128)}, /*index=5*/f32[4,1024]{1,0:T(4,128)}) custom-call(bf16[2,256,1024]{2,1,0:T(8,128)(2,1)} %get-tuple-element.15.out_i, bf16[2,256,1024]{2,1,0:T(8,128)(2,1)} %get-tuple-element.16.tg_i, ...), custom_call_target="tpu_custom_call" | custom-call | tf_op jit(solution)/shard_map/pallas_call | solution.py:672

commit v6 on v5

--- a/solution.py
+++ b/solution.py
@@ -302,9 +302,10 @@
             attend(2 * step + t)
 
     load_o.wait()
+    acc[...] = dot(on[...].reshape(2 * span, width), wo[...])
     for s in (0, 1):
         here = pl.ds(s * span, span)
-        r = tokin[s].astype(F32) + (dot(on[s], wo[...]) + row(out_bias))
+        r = tokin[s].astype(F32) + (acc[here] + row(out_bias))
         resid[here] = r
         normed, _ = norm_stats(r)
         n2[s] = (normed * row(gain2) + row(shift2)).astype(BF)
@@ -369,7 +370,9 @@
         normed, inverse = norm_stats(resid[here])
         g = ogin[s].astype(F32) + norm_back(acc[here], normed, inverse, row(gain2))
         resid[here] = g
-        n2[s] = dot(g.astype(BF), wo[...], NT).astype(BF)
+        n2[s] = g.astype(BF)
+    made_att = dot(n2[...].reshape(2 * span, width), wo[...], NT).astype(BF)
+    n2[...] = made_att.reshape(2, span, width)
 
     dk = ogin
 
@@ -453,6 +456,12 @@
                 load_e(2 * step + t - kept).start()
 
     dq = on
+    cross, near = 1 - z // 2, z // 2
+
+    @pl.loop(0, blocks)
+    def _(c):
+        here = pl.ds(pl.multiple_of(c * 256, 256), 256)
+        acc[0:span, here] = dot(dq[cross], wf[here, 0:width], NT)
 
     @pl.loop(0, pairs_n)
     def _(turn):
@@ -464,7 +473,6 @@
                 own = store[s, :, lanes].astype(F32)
                 store[s, :, lanes] = (own + part_in[hp, t, s].astype(F32)).astype(BF)
 
-    cross, near = 1 - z // 2, z // 2
     piece = span // 4
     tg = n2
 
@@ -507,13 +515,16 @@
             total.at[sender], total.at[sender], all_s.at[d - 1], all_r.at[sender], mate
         ).wait_recv()
 
-    def project_back(s, first, count):
+    def project_back(s, first, count, started):
         rows_p = slice(first, first + count)
 
         @pl.loop(0, blocks)
         def _(c):
             here = pl.ds(pl.multiple_of(c * 256, 256), 256)
-            made = dot(dq[s, rows_p], wf[here, 0:width], NT)
+            if started:
+                made = acc[rows_p, here]
+            else:
+                made = dot(dq[s, rows_p], wf[here, 0:width], NT)
             made += dot(dk[s, rows_p], wf[here, width : 2 * width], NT)
             made += dot(dv[s, rows_p], wf[here, 2 * width : 3 * width], NT)
             acc[rows_p, here] = made
@@ -523,11 +534,11 @@
         back = norm_back(acc[rows_p], normed, inverse, row(gain))
         tg[s, rows_p] = (resid[rows_s] + back).astype(BF)
 
-    project_back(cross, 0, span // 2)
+    project_back(cross, 0, span // 2, True)
     for i in (0, 1):
         out_send[i].wait_send()
     tg_copy(cross, 0).start()
-    project_back(cross, span // 2, span // 2)
+    project_back(cross, span // 2, span // 2, True)
     for k, (grad, down, up) in enumerate(((dq, down_q, up_q), (dv, down_v, up_v))):
         up_total = down_total = 0.0
         for i in (0, 1):
@@ -543,7 +554,7 @@
         spread(d).start()
     ar_in[group] = ar[group]
     tg_copy(cross, 1).start()
-    project_back(near, 0, span)
+    project_back(near, 0, span, False)
     for d in range(1, pieces):
         spread_wait(d)
     added = ar_in[0]

time: 113 us -> 112 us (level)
  no operation moved by 1% of the time
where the time goes in v6:
time: 112 us; the launch traced here: 111 us
  Pallas kernels  110 us (98%)
    pallas_call x1, Pallas kernels, on_device(): pl.pallas_call(fused, out_shape=(shape(two, BF), shape(two, BF), shape((p...  108 us
    pallas_call x1, Pallas kernels, on_device(): pl.pallas_call(deliver_kernel, grid=(slots,), out_shape=(shape(two, BF),...  2.62 us

profile of v6, /device:TPU:0, one launch (start us, length us, event | category | flops | bytes accessed | tf_op | source)
XLA Modules:
  0.0 111.2 jit_solution(7600568561086345809)
XLA Ops:
  0.6 107.8 %shard_map.226 = (bf16[2,256,1024]{2,1,0:T(8,128)(2,1)}, bf16[2,256,1024]{2,1,0:T(8,128)(2,1)}, f32[8,16,128]{2,1,0:T(8,128)}, bf16[4,2,5,256,256]{4,3,2,1,0:T(8,128)(2,1)}) custom-call(bf16[2,256,1024]{2,1,0:T(8,128)(2,1)} %refs_0_.1, bf16[2,256,1024]{2,1,0:T(8,128)(2,1)} %refs_1_.1, bf16[1024,3072]{1,0:T(8,128)(2,1)} %refs_2_.1, ...), custom_call_target="tpu_custom_call" | custom-call | tf_op jit(solution)/shard_map/pallas_call | solution.py:641
  108.4 2.6 %shard_map.227 = (bf16[2,256,1024]{2,1,0:T(8,128)(2,1)}, bf16[2,256,1024]{2,1,0:T(8,128)(2,1)}, f32[4,1024]{1,0:T(4,128)}, f32[4,1024]{1,0:T(4,128)}, f32[4,1024]{1,0:T(4,128)}, /*index=5*/f32[4,1024]{1,0:T(4,128)}) custom-call(bf16[2,256,1024]{2,1,0:T(8,128)(2,1)} %get-tuple-element.15.out_i, bf16[2,256,1024]{2,1,0:T(8,128)(2,1)} %get-tuple-element.16.tg_i, ...), custom_call_target="tpu_custom_call" | custom-call | tf_op jit(solution)/shard_map/pallas_call | solution.py:683

commit v7 on v6

--- a/solution.py
+++ b/solution.py
@@ -198,8 +198,6 @@
             for copy in tok_send:
                 copy.wait_send()
             pl.semaphore_signal(sent, inc=1, device_id=beside, device_id_type=MESH)
-        remote(tokin.at[s], tokin.at[s], tok_s.at[0], tok_r.at[s], mate).wait_recv()
-        if turn == 1:
             pl.semaphore_wait(sent, 1)
             og_send = [
                 remote(og.at[i], ogin.at[z // 2], og_s.at[i], og_r.at[z // 2], at["hosts"][i])
@@ -207,6 +205,8 @@
             ]
             for copy in og_send:
                 copy.start()
+        remote(tokin.at[s], tokin.at[s], tok_s.at[0], tok_r.at[s], mate).wait_recv()
+        if turn == 1:
             for c in (0, 1):
                 for copy in load_mlp(c):
                     copy.start()

time: 112 us -> 112 us (level)
  no operation moved by 1% of the time
where the time goes in v7:
time: 112 us; the launch traced here: 111 us
  Pallas kernels  110 us (98%)
    pallas_call x1, Pallas kernels, on_device(): pl.pallas_call(fused, out_shape=(shape(two, BF), shape(two, BF), shape((p...  108 us
    pallas_call x1, Pallas kernels, on_device(): pl.pallas_call(deliver_kernel, grid=(slots,), out_shape=(shape(two, BF),...  2.62 us

profile of v7, /device:TPU:0, one launch (start us, length us, event | category | flops | bytes accessed | tf_op | source)
XLA Modules:
  0.0 111.2 jit_solution(13205231262007911831)
XLA Ops:
  0.6 107.8 %shard_map.226 = (bf16[2,256,1024]{2,1,0:T(8,128)(2,1)}, bf16[2,256,1024]{2,1,0:T(8,128)(2,1)}, f32[8,16,128]{2,1,0:T(8,128)}, bf16[4,2,5,256,256]{4,3,2,1,0:T(8,128)(2,1)}) custom-call(bf16[2,256,1024]{2,1,0:T(8,128)(2,1)} %refs_0_.1, bf16[2,256,1024]{2,1,0:T(8,128)(2,1)} %refs_1_.1, bf16[1024,3072]{1,0:T(8,128)(2,1)} %refs_2_.1, ...), custom_call_target="tpu_custom_call" | custom-call | tf_op jit(solution)/shard_map/pallas_call | solution.py:641
  108.4 2.6 %shard_map.227 = (bf16[2,256,1024]{2,1,0:T(8,128)(2,1)}, bf16[2,256,1024]{2,1,0:T(8,128)(2,1)}, f32[4,1024]{1,0:T(4,128)}, f32[4,1024]{1,0:T(4,128)}, f32[4,1024]{1,0:T(4,128)}, /*index=5*/f32[4,1024]{1,0:T(4,128)}) custom-call(bf16[2,256,1024]{2,1,0:T(8,128)(2,1)} %get-tuple-element.15.out_i, bf16[2,256,1024]{2,1,0:T(8,128)(2,1)} %get-tuple-element.16.tg_i, ...), custom_call_target="tpu_custom_call" | custom-call | tf_op jit(solution)/shard_map/pallas_call | solution.py:683
